TPU v7x, 128 devices: a whole 4x4x4 slice. The times are simulated.
128 devices in a mesh: wide: 32 (over x, z, core), narrow: 4 (over y).
Axes of the slice: x: 4, y: 4, z: 4, core: 2. Of those that a mesh axis runs over, the one named last changes fastest.
Arguments:
- points: bfloat16 [4, 512, 8, 512], P('narrow', 'wide'), may hold values from -1.5 to 1.5
- charges: bfloat16 [4, 512, 32, 512], P('narrow', 'wide'), may hold values from -6 to 6
- leaf_interp_basis: bfloat16 [4, 512, 512, 128], P('narrow', 'wide'), may hold values from -0.25 to 0.25
- leaf_skeleton: int32 [4, 512, 128], P('narrow', 'wide'), may hold values from 0 to 511, as said below
- local_transfer: bfloat16 [4, 480, 256, 128], P('narrow', 'wide'), may hold values from -0.5 to 0.5
- local_skeleton: int32 [4, 480, 128], P('narrow', 'wide'), may hold values from 0 to 255, as said below
- top_transfer: bfloat16 [4, 31, 256, 128], P('narrow'), may hold values from -0.5 to 0.5
- top_skeleton: int32 [4, 31, 128], P('narrow'), may hold values from 0 to 255, as said below
- near_list: int32 [4, 512, 8], P('narrow', 'wide'), may hold values from 0 to 511, as said below
- far_list: int32 [4, 32, 4], P('narrow', 'wide'), may hold values from 0 to 127, as said below
Outputs:
- potentials: bfloat16 [4, 512, 32, 512], P('narrow', 'wide')
Inputs may be any that keep to these rules, and one draw needn't show every extreme that they name: `leaf_skeleton`: each row names 128 different points of its leaf. `local_skeleton`: each row names 128 different columns of the children's joined skeletons. `top_skeleton`: each row names 128 different columns of the children's joined skeletons. `near_list`: the row of leaf m starts with m and holds 8 different leaves of the same group, each within 16 of m. `far_list`: each row names 4 different device nodes; the first is the node of the row's own group at position (i + 16) mod 32 for row position i, the others belong to other groups.
All inputs are finite; a program needn't handle non-finite values.
Results may differ from a plain program's by a relative error of at most 0.00205.
Values may be sent and summed in bfloat16 or wider, within the bound.
A program may use at most 64 MiB of HBM per device.

v0:
```python
import math

import jax
import jax.numpy as jnp
from jax import lax
from jax.sharding import PartitionSpec as P

inv_width = 1.5
topmost_level = lax.Precision.HIGHEST


def with_halo(block, sides, width):
    for axis, dim in sides:
        count = lax.axis_size(axis)
        forward = [(i, i + 1) for i in range(count - 1)]
        backward = [(target, source) for source, target in forward]
        low = lax.ppermute(
            lax.slice_in_dim(block, block.shape[dim] - width, None, axis=dim), axis, forward
        )
        high = lax.ppermute(lax.slice_in_dim(block, 0, width, axis=dim), axis, backward)
        block = jnp.concatenate([low, block, high], axis=dim)
    return block


def from_partner(block, axis, stride):
    count = lax.axis_size(axis)
    route = []
    for low in range(count):
        high = low | 1 << stride
        if high != low and high < count:
            route += [(low, high), (high, low)]
    return lax.ppermute(block, axis, route)


def gaussian(source_points, target_points):
    cross = jnp.einsum("...dn,...dm->...nm", source_points, target_points, precision=topmost_level)
    source_sq = jnp.sum(source_points * source_points, axis=-2)
    target_sq = jnp.sum(target_points * target_points, axis=-2)
    return jnp.exp(-inv_width * (source_sq[..., :, None] + target_sq[..., None, :] - 2.0 * cross))


def select_columns(values, chosen):
    table = (chosen[:, None, :] == jnp.arange(values.shape[2])[None, :, None]).astype(jnp.float32)
    return jnp.einsum("mdt,mts->mds", values, table, precision=topmost_level)


def merge_up(left_node, right_node, transfer, chosen, rhs_count):
    joined = jnp.concatenate([left_node, right_node], axis=2)
    charge_weight = jnp.einsum(
        "mrt,mts->mrs", joined[:, :rhs_count], transfer.astype(jnp.float32), precision=topmost_level
    )
    coords = select_columns(joined[:, rhs_count:], chosen)
    return jnp.concatenate([charge_weight, coords], axis=1)


def push_down(potential_field, transfer):
    parents = potential_field.shape[0]
    children = jnp.einsum(
        "mrs,mts->mrt", potential_field, transfer.astype(jnp.float32), precision=topmost_level
    )
    children = children.reshape(parents, potential_field.shape[1], 2, potential_field.shape[2])
    return jnp.transpose(children, (0, 2, 1, 3)).reshape(
        2 * parents, potential_field.shape[1], potential_field.shape[2]
    )


def fetch_roots(group_root):
    return lax.all_gather(group_root[None], "narrow", axis=0, tiled=True)


def shards(
    points,
    charges,
    leaf_interp_basis,
    leaf_skeleton,
    local_transfer,
    local_skeleton,
    top_transfer,
    top_skeleton,
    near_list,
    far_list,
):
    wide_count = lax.axis_size("wide")
    group_count = lax.axis_size("narrow")
    point_location = lax.axis_index("wide")
    group_index = lax.axis_index("narrow")
    leaf_dev = points.shape[1]
    dim_count = points.shape[2]
    box_size = points.shape[3]
    rhs_count = charges.shape[2]
    skel_count = leaf_interp_basis.shape[3]
    local_levels = leaf_dev.bit_length() - 1
    top_levels = wide_count.bit_length() - 1
    pair_rows = jnp.concatenate([points, charges], axis=2)
    wide_pair = with_halo(pair_rows, (("wide", 1),), leaf_dev)[0]
    charge_weight = jnp.einsum(
        "xqn,xna->xqa", charges[0], leaf_interp_basis[0], preferred_element_type=jnp.float32
    )
    point_table = (leaf_skeleton[0][:, None, :] == jnp.arange(box_size)[None, :, None]).astype(
        jnp.bfloat16
    )
    skeleton_points = jnp.einsum(
        "xdn,xns->xds", points[0], point_table, preferred_element_type=jnp.float32
    )
    level_nodes = jnp.concatenate([charge_weight, skeleton_points], axis=1)
    for section in range(local_levels):
        parents = leaf_dev >> section + 1
        level_nodes = merge_up(
            level_nodes[0::2],
            level_nodes[1::2],
            local_transfer[0, parents - 1 : 2 * parents - 1],
            local_skeleton[0, parents - 1 : 2 * parents - 1],
            rhs_count,
        )
    own_node = level_nodes[0]
    every_node = lax.all_gather(own_node[None], ("wide", "narrow"), axis=0, tiled=True)
    far_ids = far_list[0, 0]
    node_rows = far_ids % wide_count * group_count + far_ids // wide_count
    node_table = (node_rows[:, None] == jnp.arange(every_node.shape[0])[None, :]).astype(
        jnp.float32
    )
    sources = jnp.einsum("fe,ers->frs", node_table, every_node, precision=topmost_level)
    kernel_block = gaussian(sources[:, rhs_count:], own_node[None, rhs_count:])
    far_node = jnp.einsum(
        "frn,fnm->rm", sources[:, :rhs_count], kernel_block, precision=topmost_level
    )
    current = own_node
    for section in range(top_levels):
        partner = from_partner(current, "wide", section)
        side_bit = point_location >> section & 1
        left_node = jnp.where(side_bit == 1, partner, current)
        right_node = jnp.where(side_bit == 1, current, partner)
        heap_slot = (wide_count >> section + 1) - 1 + (point_location >> section + 1)
        transfer = lax.dynamic_index_in_dim(top_transfer[0], heap_slot, 0, keepdims=True)
        chosen = lax.dynamic_index_in_dim(top_skeleton[0], heap_slot, 0, keepdims=True)
        current = merge_up(left_node[None], right_node[None], transfer, chosen, rhs_count)[0]
    all_roots = fetch_roots(current)
    other_mask = (jnp.arange(group_count) != group_index).astype(jnp.float32)
    root_kernel = gaussian(all_roots[:, rhs_count:], current[None, rhs_count:])
    top_field = jnp.einsum(
        "grn,gnm,g->rm", all_roots[:, :rhs_count], root_kernel, other_mask, precision=topmost_level
    )
    for section in reversed(range(top_levels)):
        heap_slot = (wide_count >> section + 1) - 1 + (point_location >> section + 1)
        side_bit = point_location >> section & 1
        transfer = lax.dynamic_index_in_dim(top_transfer[0], heap_slot, 0, keepdims=False)
        lower_block = lax.dynamic_slice_in_dim(transfer, side_bit * skel_count, skel_count, 0)
        top_field = jnp.einsum(
            "rs,ts->rt", top_field, lower_block.astype(jnp.float32), precision=topmost_level
        )
    potential_field = (top_field + far_node)[None]
    for section in reversed(range(local_levels)):
        parents = leaf_dev >> section + 1
        potential_field = push_down(
            potential_field, local_transfer[0, parents - 1 : 2 * parents - 1]
        )
    distant_output = jnp.einsum(
        "vcp,vfp->vcf",
        potential_field,
        leaf_interp_basis[0].astype(jnp.float32),
        precision=topmost_level,
    )
    first_leaf = point_location * leaf_dev - leaf_dev
    box_rows = wide_pair.shape[0]
    flat_pair = wide_pair.reshape(box_rows, (dim_count + rhs_count) * box_size)

    def near_leaf(leaf_args):
        leaf_ids, target_points = leaf_args
        pick_table = ((leaf_ids - first_leaf)[:, None] == jnp.arange(box_rows)[None, :]).astype(
            jnp.bfloat16
        )
        block_rows = jnp.dot(pick_table, flat_pair, preferred_element_type=jnp.float32).astype(
            jnp.bfloat16
        )
        block_rows = block_rows.reshape(leaf_ids.shape[0], dim_count + rhs_count, box_size)
        source_points = block_rows[:, :dim_count]
        source_charge = block_rows[:, dim_count:]
        cross = jnp.einsum(
            "kdn,dm->knm", source_points, target_points, preferred_element_type=jnp.float32
        )
        source_wide = source_points.astype(jnp.float32)
        target_wide = target_points.astype(jnp.float32)
        source_sq = jnp.sum(source_wide * source_wide, axis=1)
        target_sq = jnp.sum(target_wide * target_wide, axis=0)
        near_kernel = jnp.exp(
            -inv_width * (source_sq[:, :, None] + target_sq[None, None, :] - 2.0 * cross)
        ).astype(jnp.bfloat16)
        return jnp.einsum(
            "kcn,knm->cm", source_charge, near_kernel, preferred_element_type=jnp.float32
        )

    near_out = lax.map(near_leaf, (near_list[0], points[0]))
    out_scale = 1.0 / math.sqrt(box_size)
    return ((near_out + distant_output) * out_scale).astype(jnp.bfloat16)[None]


def solution(mesh):
    return jax.shard_map(
        shards,
        mesh=mesh,
        in_specs=(
            P("narrow", "wide", None, None),
            P("narrow", "wide", None, None),
            P("narrow", "wide", None, None),
            P("narrow", "wide", None),
            P("narrow", "wide", None, None),
            P("narrow", "wide", None),
            P("narrow", None, None, None),
            P("narrow", None, None),
            P("narrow", "wide", None),
            P("narrow", "wide", None),
        ),
        out_specs=P("narrow", "wide", None, None),
        check_vma=False,
    )
```

profile of v0, /device:TPU:0, one launch (start us, length us, event | category | flops | bytes accessed | tf_op | source)
XLA Modules:
  0.0 213.8 jit_solution(16852861284422997112)
XLA Ops:
  8.1 1.5 fusion.24
  16.5 2.1 collective-permute-start.3
  21.5 4.0 %collective-permute-start.4 = (f32[40,128]{1,0:T(8,128)S(1)}, f32[40,128]{1,0:T(8,128)S(1)}, u32[]{:S(2)}, u32[]{:S(2)}) collective-permute-start(f32[40,128]{1,0:T(8,128)S(1)} %maximum_bitcast_fusion.1), channel_id=1, source_target_pairs={{0,16},{16,0},{4,20},{20,4},{8,24},{24,8},{12,28},{28,12},{32,48},... | collective-permute-start | bytes 61448 | tf_op jit(solution)/shard_map/ppermute | solution.py:32
  25.5 1.9 constant_dynamic-update-slice_fusion
  27.4 2.1 collective-permute-start
  32.0 5.8 %collective-permute-start.5 = (f32[40,128]{1,0:T(8,128)S(1)}, f32[40,128]{1,0:T(8,128)S(1)}, u32[]{:S(2)}, u32[]{:S(2)}) collective-permute-start(f32[40,128]{1,0:T(8,128)S(1)} %maximum_bitcast_fusion.2), channel_id=1, source_target_pairs={{0,32},{32,0},{4,36},{36,4},{8,40},{40,8},{12,44},{44,12},{16,48},... | collective-permute-start | bytes 61448 | tf_op jit(solution)/shard_map/ppermute | solution.py:32
  38.3 7.4 %collective-permute-done.5 = f32[40,128]{1,0:T(8,128)S(1)} collective-permute-done((f32[40,128]{1,0:T(8,128)S(1)}, f32[40,128]{1,0:T(8,128)S(1)}, u32[]{:S(2)}, u32[]{:S(2)}) %collective-permute-start.5) | collective-permute-done | bytes 20512 | tf_op jit(solution)/shard_map/ppermute | solution.py:32
  46.9 2.8 %collective-permute-start.6 = (f32[40,128]{1,0:T(8,128)S(1)}, f32[40,128]{1,0:T(8,128)S(1)}, u32[]{:S(2)}, u32[]{:S(2)}) collective-permute-start(f32[40,128]{1,0:T(8,128)S(1)} %maximum_bitcast_fusion.3), channel_id=1, source_target_pairs={{0,64},{64,0},{4,68},{68,4},{8,72},{72,8},{12,76},{76,12},{16,80},... | collective-permute-start | bytes 61448 | tf_op jit(solution)/shard_map/ppermute | solution.py:32
  50.3 1.9 collective-permute-done.6
  53.4 12.6 %all_gather.6 = f32[4,40,128]{2,1,0:T(8,128)S(1)} all-gather(f32[1,40,128]{2,1,0:T(8,128)S(1)} %pad_maximum_fusion.13), channel_id=1, replica_groups=mesh['wide'=32,'narrow'=4] {'narrow'}, dimensions={0}, use_global_device_ids=true | all-gather | bytes 102400 | tf_op jit(solution)/shard_map/all_gather | solution.py:68
  70.8 1.6 fusion.117
  72.3 1.7 pad_maximum_fusion
  74.0 2.0 copy.21
  76.0 122.5 %while.10 = (s32[]{:T(128)}, f32[16,32,512]{2,1,0:T(8,128)}, s32[16,8]{1,0:T(8,128)}, s32[]{:T(128)}, bf16[48,20480]{1,0:T(8,128)(2,1)}, /*index=5*/bf16[16,8,512]{2,1,0:T(8,128)(2,1)S(1)}, s32[]{:T(128)}) while((s32[]{:T(128)}, f32[16,32,512]{2,1,0:T(8,128)}, s32[16,8]{1,0:T(8,128)}, s32[]{:T(128)}, bf16[48,20480]{1,0:T(8,128)(2,1)}, ...), condition=%wide.region_3.4_spmd, body=%wide.region_0.3_spmd.sunk | while | flops 194256784 | bytes 3462329 | solution.py:192
  76.7 2.0 convolution_convert_fusion.2
  79.4 4.3 %fusion.230 = f32[16,32,512]{2,1,0:T(8,128)} fusion(f32[16,32,512]{2,1,0:T(8,128)} %get-tuple-element.142, s32[]{:T(128)} %get-tuple-element.141, f32[512]{0:T(512)} %multiply_reduce_fusion.8, f32[8,512]{1,0:T(8,128)S(1)} %multiply_reduce_fusion.9, bf16[8,32,512]{2,0,1:T(8,128)(2,1)S(1)} %slice.358, bf16[8,8,512]{2,0,1:T(8,128)(2,1)S(1)} %slice.359, ...), kind=kOutput, calls=%fused_computation.5.clone.1 | convolution fusion | flops 178257920 | bytes 420864 | tf_op jit(solution)/shard_map/while/body/eval_jaxpr/kcn,knm->cm/dot_general | solution.py:188
  84.4 2.0 convolution_convert_fusion.2
  87.0 4.3 %fusion.230 = f32[16,32,512]{2,1,0:T(8,128)} fusion(f32[16,32,512]{2,1,0:T(8,128)} %get-tuple-element.142, s32[]{:T(128)} %get-tuple-element.141, f32[512]{0:T(512)} %multiply_reduce_fusion.8, f32[8,512]{1,0:T(8,128)S(1)} %multiply_reduce_fusion.9, bf16[8,32,512]{2,0,1:T(8,128)(2,1)S(1)} %slice.358, bf16[8,8,512]{2,0,1:T(8,128)(2,1)S(1)} %slice.359, ...), kind=kOutput, calls=%fused_computation.5.clone.1 | convolution fusion | flops 178257920 | bytes 420864 | tf_op jit(solution)/shard_map/while/body/eval_jaxpr/kcn,knm->cm/dot_general | solution.py:188
  92.0 2.0 convolution_convert_fusion.2
  94.7 4.3 %fusion.230 = f32[16,32,512]{2,1,0:T(8,128)} fusion(f32[16,32,512]{2,1,0:T(8,128)} %get-tuple-element.142, s32[]{:T(128)} %get-tuple-element.141, f32[512]{0:T(512)} %multiply_reduce_fusion.8, f32[8,512]{1,0:T(8,128)S(1)} %multiply_reduce_fusion.9, bf16[8,32,512]{2,0,1:T(8,128)(2,1)S(1)} %slice.358, bf16[8,8,512]{2,0,1:T(8,128)(2,1)S(1)} %slice.359, ...), kind=kOutput, calls=%fused_computation.5.clone.1 | convolution fusion | flops 178257920 | bytes 420864 | tf_op jit(solution)/shard_map/while/body/eval_jaxpr/kcn,knm->cm/dot_general | solution.py:188
  99.7 2.0 convolution_convert_fusion.2
  102.4 4.3 %fusion.230 = f32[16,32,512]{2,1,0:T(8,128)} fusion(f32[16,32,512]{2,1,0:T(8,128)} %get-tuple-element.142, s32[]{:T(128)} %get-tuple-element.141, f32[512]{0:T(512)} %multiply_reduce_fusion.8, f32[8,512]{1,0:T(8,128)S(1)} %multiply_reduce_fusion.9, bf16[8,32,512]{2,0,1:T(8,128)(2,1)S(1)} %slice.358, bf16[8,8,512]{2,0,1:T(8,128)(2,1)S(1)} %slice.359, ...), kind=kOutput, calls=%fused_computation.5.clone.1 | convolution fusion | flops 178257920 | bytes 420864 | tf_op jit(solution)/shard_map/while/body/eval_jaxpr/kcn,knm->cm/dot_general | solution.py:188
  107.4 2.0 convolution_convert_fusion.2
  110.0 4.3 %fusion.230 = f32[16,32,512]{2,1,0:T(8,128)} fusion(f32[16,32,512]{2,1,0:T(8,128)} %get-tuple-element.142, s32[]{:T(128)} %get-tuple-element.141, f32[512]{0:T(512)} %multiply_reduce_fusion.8, f32[8,512]{1,0:T(8,128)S(1)} %multiply_reduce_fusion.9, bf16[8,32,512]{2,0,1:T(8,128)(2,1)S(1)} %slice.358, bf16[8,8,512]{2,0,1:T(8,128)(2,1)S(1)} %slice.359, ...), kind=kOutput, calls=%fused_computation.5.clone.1 | convolution fusion | flops 178257920 | bytes 420864 | tf_op jit(solution)/shard_map/while/body/eval_jaxpr/kcn,knm->cm/dot_general | solution.py:188
  115.0 2.0 convolution_convert_fusion.2
  117.7 4.3 %fusion.230 = f32[16,32,512]{2,1,0:T(8,128)} fusion(f32[16,32,512]{2,1,0:T(8,128)} %get-tuple-element.142, s32[]{:T(128)} %get-tuple-element.141, f32[512]{0:T(512)} %multiply_reduce_fusion.8, f32[8,512]{1,0:T(8,128)S(1)} %multiply_reduce_fusion.9, bf16[8,32,512]{2,0,1:T(8,128)(2,1)S(1)} %slice.358, bf16[8,8,512]{2,0,1:T(8,128)(2,1)S(1)} %slice.359, ...), kind=kOutput, calls=%fused_computation.5.clone.1 | convolution fusion | flops 178257920 | bytes 420864 | tf_op jit(solution)/shard_map/while/body/eval_jaxpr/kcn,knm->cm/dot_general | solution.py:188
  122.7 2.0 convolution_convert_fusion.2
  125.3 4.3 %fusion.230 = f32[16,32,512]{2,1,0:T(8,128)} fusion(f32[16,32,512]{2,1,0:T(8,128)} %get-tuple-element.142, s32[]{:T(128)} %get-tuple-element.141, f32[512]{0:T(512)} %multiply_reduce_fusion.8, f32[8,512]{1,0:T(8,128)S(1)} %multiply_reduce_fusion.9, bf16[8,32,512]{2,0,1:T(8,128)(2,1)S(1)} %slice.358, bf16[8,8,512]{2,0,1:T(8,128)(2,1)S(1)} %slice.359, ...), kind=kOutput, calls=%fused_computation.5.clone.1 | convolution fusion | flops 178257920 | bytes 420864 | tf_op jit(solution)/shard_map/while/body/eval_jaxpr/kcn,knm->cm/dot_general | solution.py:188
  130.3 2.0 convolution_convert_fusion.2
  133.0 4.3 %fusion.230 = f32[16,32,512]{2,1,0:T(8,128)} fusion(f32[16,32,512]{2,1,0:T(8,128)} %get-tuple-element.142, s32[]{:T(128)} %get-tuple-element.141, f32[512]{0:T(512)} %multiply_reduce_fusion.8, f32[8,512]{1,0:T(8,128)S(1)} %multiply_reduce_fusion.9, bf16[8,32,512]{2,0,1:T(8,128)(2,1)S(1)} %slice.358, bf16[8,8,512]{2,0,1:T(8,128)(2,1)S(1)} %slice.359, ...), kind=kOutput, calls=%fused_computation.5.clone.1 | convolution fusion | flops 178257920 | bytes 420864 | tf_op jit(solution)/shard_map/while/body/eval_jaxpr/kcn,knm->cm/dot_general | solution.py:188
  138.0 2.0 convolution_convert_fusion.2
  140.6 4.3 %fusion.230 = f32[16,32,512]{2,1,0:T(8,128)} fusion(f32[16,32,512]{2,1,0:T(8,128)} %get-tuple-element.142, s32[]{:T(128)} %get-tuple-element.141, f32[512]{0:T(512)} %multiply_reduce_fusion.8, f32[8,512]{1,0:T(8,128)S(1)} %multiply_reduce_fusion.9, bf16[8,32,512]{2,0,1:T(8,128)(2,1)S(1)} %slice.358, bf16[8,8,512]{2,0,1:T(8,128)(2,1)S(1)} %slice.359, ...), kind=kOutput, calls=%fused_computation.5.clone.1 | convolution fusion | flops 178257920 | bytes 420864 | tf_op jit(solution)/shard_map/while/body/eval_jaxpr/kcn,knm->cm/dot_general | solution.py:188
  145.7 2.0 convolution_convert_fusion.2
  148.3 4.3 %fusion.230 = f32[16,32,512]{2,1,0:T(8,128)} fusion(f32[16,32,512]{2,1,0:T(8,128)} %get-tuple-element.142, s32[]{:T(128)} %get-tuple-element.141, f32[512]{0:T(512)} %multiply_reduce_fusion.8, f32[8,512]{1,0:T(8,128)S(1)} %multiply_reduce_fusion.9, bf16[8,32,512]{2,0,1:T(8,128)(2,1)S(1)} %slice.358, bf16[8,8,512]{2,0,1:T(8,128)(2,1)S(1)} %slice.359, ...), kind=kOutput, calls=%fused_computation.5.clone.1 | convolution fusion | flops 178257920 | bytes 420864 | tf_op jit(solution)/shard_map/while/body/eval_jaxpr/kcn,knm->cm/dot_general | solution.py:188
  153.3 2.0 convolution_convert_fusion.2
  156.0 4.3 %fusion.230 = f32[16,32,512]{2,1,0:T(8,128)} fusion(f32[16,32,512]{2,1,0:T(8,128)} %get-tuple-element.142, s32[]{:T(128)} %get-tuple-element.141, f32[512]{0:T(512)} %multiply_reduce_fusion.8, f32[8,512]{1,0:T(8,128)S(1)} %multiply_reduce_fusion.9, bf16[8,32,512]{2,0,1:T(8,128)(2,1)S(1)} %slice.358, bf16[8,8,512]{2,0,1:T(8,128)(2,1)S(1)} %slice.359, ...), kind=kOutput, calls=%fused_computation.5.clone.1 | convolution fusion | flops 178257920 | bytes 420864 | tf_op jit(solution)/shard_map/while/body/eval_jaxpr/kcn,knm->cm/dot_general | solution.py:188
  160.9 2.0 convolution_convert_fusion.2
  163.6 4.3 %fusion.230 = f32[16,32,512]{2,1,0:T(8,128)} fusion(f32[16,32,512]{2,1,0:T(8,128)} %get-tuple-element.142, s32[]{:T(128)} %get-tuple-element.141, f32[512]{0:T(512)} %multiply_reduce_fusion.8, f32[8,512]{1,0:T(8,128)S(1)} %multiply_reduce_fusion.9, bf16[8,32,512]{2,0,1:T(8,128)(2,1)S(1)} %slice.358, bf16[8,8,512]{2,0,1:T(8,128)(2,1)S(1)} %slice.359, ...), kind=kOutput, calls=%fused_computation.5.clone.1 | convolution fusion | flops 178257920 | bytes 420864 | tf_op jit(solution)/shard_map/while/body/eval_jaxpr/kcn,knm->cm/dot_general | solution.py:188
  168.6 2.0 convolution_convert_fusion.2
  171.3 4.3 %fusion.230 = f32[16,32,512]{2,1,0:T(8,128)} fusion(f32[16,32,512]{2,1,0:T(8,128)} %get-tuple-element.142, s32[]{:T(128)} %get-tuple-element.141, f32[512]{0:T(512)} %multiply_reduce_fusion.8, f32[8,512]{1,0:T(8,128)S(1)} %multiply_reduce_fusion.9, bf16[8,32,512]{2,0,1:T(8,128)(2,1)S(1)} %slice.358, bf16[8,8,512]{2,0,1:T(8,128)(2,1)S(1)} %slice.359, ...), kind=kOutput, calls=%fused_computation.5.clone.1 | convolution fusion | flops 178257920 | bytes 420864 | tf_op jit(solution)/shard_map/while/body/eval_jaxpr/kcn,knm->cm/dot_general | solution.py:188
  176.3 2.0 convolution_convert_fusion.2
  178.9 4.3 %fusion.230 = f32[16,32,512]{2,1,0:T(8,128)} fusion(f32[16,32,512]{2,1,0:T(8,128)} %get-tuple-element.142, s32[]{:T(128)} %get-tuple-element.141, f32[512]{0:T(512)} %multiply_reduce_fusion.8, f32[8,512]{1,0:T(8,128)S(1)} %multiply_reduce_fusion.9, bf16[8,32,512]{2,0,1:T(8,128)(2,1)S(1)} %slice.358, bf16[8,8,512]{2,0,1:T(8,128)(2,1)S(1)} %slice.359, ...), kind=kOutput, calls=%fused_computation.5.clone.1 | convolution fusion | flops 178257920 | bytes 420864 | tf_op jit(solution)/shard_map/while/body/eval_jaxpr/kcn,knm->cm/dot_general | solution.py:188
  183.9 2.0 convolution_convert_fusion.2
  186.6 4.3 %fusion.230 = f32[16,32,512]{2,1,0:T(8,128)} fusion(f32[16,32,512]{2,1,0:T(8,128)} %get-tuple-element.142, s32[]{:T(128)} %get-tuple-element.141, f32[512]{0:T(512)} %multiply_reduce_fusion.8, f32[8,512]{1,0:T(8,128)S(1)} %multiply_reduce_fusion.9, bf16[8,32,512]{2,0,1:T(8,128)(2,1)S(1)} %slice.358, bf16[8,8,512]{2,0,1:T(8,128)(2,1)S(1)} %slice.359, ...), kind=kOutput, calls=%fused_computation.5.clone.1 | convolution fusion | flops 178257920 | bytes 420864 | tf_op jit(solution)/shard_map/while/body/eval_jaxpr/kcn,knm->cm/dot_general | solution.py:188
  191.6 2.0 convolution_convert_fusion.2
  194.2 4.3 %fusion.230 = f32[16,32,512]{2,1,0:T(8,128)} fusion(f32[16,32,512]{2,1,0:T(8,128)} %get-tuple-element.142, s32[]{:T(128)} %get-tuple-element.141, f32[512]{0:T(512)} %multiply_reduce_fusion.8, f32[8,512]{1,0:T(8,128)S(1)} %multiply_reduce_fusion.9, bf16[8,32,512]{2,0,1:T(8,128)(2,1)S(1)} %slice.358, bf16[8,8,512]{2,0,1:T(8,128)(2,1)S(1)} %slice.359, ...), kind=kOutput, calls=%fused_computation.5.clone.1 | convolution fusion | flops 178257920 | bytes 420864 | tf_op jit(solution)/shard_map/while/body/eval_jaxpr/kcn,knm->cm/dot_general | solution.py:188
  198.6 2.9 %fusion.20 = f32[4,40,128]{2,0,1:T(4,128)S(1)} fusion(f32[128,40,128]{2,1,0:T(8,128)} %all-gather.2.cloned.1.call-done, s32[4]{0:T(128)} %fusion.172), kind=kOutput, calls=%fused_computation.22 | convolution fusion | flops 31457792 | bytes 2703376 | tf_op jit(solution)/shard_map/fe,ers->frs/dot_general | solution.py:122
  204.0 3.0 %fusion.36 = bf16[1,16,32,512]{3,2,1,0:T(8,128)(2,1)} fusion(f32[16,32,512]{2,1,0:T(8,128)S(1)} %copy-done.2, f32[16,32,128]{2,1,0:T(8,128)S(1)} %bitcast.289, bf16[1,16,512,128]{3,2,1,0:T(8,128)(2,1)S(1)} %copy-done), kind=kOutput, calls=%fused_computation.33 | convolution fusion | flops 403439616 | bytes 3932160 | tf_op jit(solution)/shard_map/vcp,vfp->vcf/dot_general | solution.py:157
  (186 shorter events, 46.0 us)
Async XLA Ops:
  6.5 1.6 copy-start
  6.5 3.1 %copy-start.9 = (s32[1,16,128]{2,1,0:T(8,128)S(1)}, s32[1,16,128]{2,1,0:T(8,128)}, u32[]{:S(2)}) copy-start(s32[1,16,128]{2,1,0:T(8,128)} %param.15) | copy-start | bytes 24580
  6.5 3.1 %copy-start.3 = (bf16[1,16,8,512]{3,2,1,0:T(8,128)(2,1)S(1)}, bf16[1,16,8,512]{3,2,1,0:T(8,128)(2,1)}, u32[]{:S(2)}) copy-start(bf16[1,16,8,512]{3,2,1,0:T(8,128)(2,1)} %param.12) | copy-start | bytes 393220
  6.5 192.0 %all-gather.2.cloned.1.call-start = ((), (), s32[]{:S(2)}) async-start(), calls=%async_computation | async-start | bytes 2641920 | tf_op jit(solution)/shard_map/all_gather | solution.py:116
  9.6 1.2 copy-start.1
  9.6 1.5 slice-start.1
  10.4 1.5 slice-start.2
  10.5 1.9 slice-start.3
  11.7 26.1 %copy-start.10 = (s32[1,1,4]{2,1,0:T(1,128)S(1)}, s32[1,1,4]{2,1,0:T(1,128)}, u32[]{:S(2)}) copy-start(s32[1,1,4]{2,1,0:T(1,128)} %param.21) | copy-start | bytes 52
  11.9 37.8 %copy-start.7 = (s32[1,16,8]{1,2,0:T(8,128)S(1)}, s32[1,16,8]{1,2,0:T(8,128)}, u32[]{:S(2)}) copy-start(s32[1,16,8]{1,2,0:T(8,128)} %param.20) | copy-start | bytes 1540
  13.5 2.8 %copy-start.5 = (f32[8,128]{1,0:T(8,128)}, f32[8,128]{1,0:T(8,128)S(1)}, u32[]{:S(2)}) copy-start(f32[8,128]{1,0:T(8,128)S(1)} %get-tuple-element.96) | copy-start | bytes 12292
  14.1 1.2 collective-permute-start.2
  16.5 3.8 %collective-permute-start.3 = (f32[40,128]{1,0:T(8,128)S(1)}, f32[40,128]{1,0:T(8,128)S(1)}, u32[]{:S(2)}, u32[]{:S(2)}) collective-permute-start(f32[40,128]{1,0:T(8,128)S(1)} %maximum_bitcast_fusion), channel_id=1, source_target_pairs={{0,8},{8,0},{4,12},{12,4},{16,24},{24,16},{20,28},{28,20},{32,40},... | collective-permute-start | bytes 61448 | tf_op jit(solution)/shard_map/ppermute | solution.py:32
  21.5 9.3 %collective-permute-start.4 = (f32[40,128]{1,0:T(8,128)S(1)}, f32[40,128]{1,0:T(8,128)S(1)}, u32[]{:S(2)}, u32[]{:S(2)}) collective-permute-start(f32[40,128]{1,0:T(8,128)S(1)} %maximum_bitcast_fusion.1), channel_id=1, source_target_pairs={{0,16},{16,0},{4,20},{20,4},{8,24},{24,8},{12,28},{28,12},{32,48},... | collective-permute-start | bytes 61448 | tf_op jit(solution)/shard_map/ppermute | solution.py:32
  27.4 44.9 %collective-permute-start = (bf16[1,16,40,512]{3,2,1,0:T(8,128)(2,1)}, bf16[1,16,40,512]{3,2,1,0:T(8,128)(2,1)}, u32[]{:S(2)}, u32[]{:S(2)}) collective-permute-start(bf16[1,16,40,512]{3,2,1,0:T(8,128)(2,1)} %constant_dynamic-update-slice_fusion), channel_id=1, source_target_pairs={{0,4},{4,8},{8,12},{12,16},{16,20},{20,24},{24,28},{28,32},{32,36}... | collective-permute-start | bytes 1966088 | tf_op jit(solution)/shard_map/ppermute | solution.py:17
  29.5 42.8 %collective-permute-start.1 = (bf16[1,16,40,512]{3,2,1,0:T(8,128)(2,1)}, bf16[1,16,40,512]{3,2,1,0:T(8,128)(2,1)}, u32[]{:S(2)}, u32[]{:S(2)}) collective-permute-start(bf16[1,16,40,512]{3,2,1,0:T(8,128)(2,1)} %constant_dynamic-update-slice_fusion), channel_id=1, source_target_pairs={{4,0},{8,4},{12,8},{16,12},{20,16},{24,20},{28,24},{32,28},{36,32}... | collective-permute-start | bytes 1966088 | tf_op jit(solution)/shard_map/ppermute | solution.py:20
  32.0 13.7 %collective-permute-start.5 = (f32[40,128]{1,0:T(8,128)S(1)}, f32[40,128]{1,0:T(8,128)S(1)}, u32[]{:S(2)}, u32[]{:S(2)}) collective-permute-start(f32[40,128]{1,0:T(8,128)S(1)} %maximum_bitcast_fusion.2), channel_id=1, source_target_pairs={{0,32},{32,0},{4,36},{36,4},{8,40},{40,8},{12,44},{44,12},{16,48},... | collective-permute-start | bytes 61448 | tf_op jit(solution)/shard_map/ppermute | solution.py:32
  46.9 5.3 %collective-permute-start.6 = (f32[40,128]{1,0:T(8,128)S(1)}, f32[40,128]{1,0:T(8,128)S(1)}, u32[]{:S(2)}, u32[]{:S(2)}) collective-permute-start(f32[40,128]{1,0:T(8,128)S(1)} %maximum_bitcast_fusion.3), channel_id=1, source_target_pairs={{0,64},{64,0},{4,68},{68,4},{8,72},{72,8},{12,76},{76,12},{16,80},... | collective-permute-start | bytes 61448 | tf_op jit(solution)/shard_map/ppermute | solution.py:32
  198.5 3.0 %copy-start.6 = (f32[8,128]{1,0:T(8,128)S(1)}, f32[8,128]{1,0:T(8,128)}, u32[]{:S(2)}) copy-start(f32[8,128]{1,0:T(8,128)} %copy-done.5) | copy-start | bytes 12292
  198.5 3.0 %copy-start.8 = (f32[128]{0:T(128)S(1)}, f32[128]{0:T(128)}, u32[]{:S(2)}) copy-start(f32[128]{0:T(128)} %get-tuple-element.95) | copy-start | bytes 1540
  198.5 3.6 %copy-start.4 = (f32[32,128]{1,0:T(8,128)S(1)}, f32[32,128]{1,0:T(8,128)}, u32[]{:S(2)}) copy-start(f32[32,128]{1,0:T(8,128)} %fusion.117) | copy-start | bytes 49156
  198.6 3.9 %slice-start = ((bf16[1,15,256,128]{3,2,1,0:T(8,128)(2,1)}), bf16[1,1,256,128]{3,2,1,0:T(8,128)(2,1)S(1)}, s32[]{:S(2)}) async-start(bf16[1,15,256,128]{3,2,1,0:T(8,128)(2,1)} %param.16), calls=%async_computation.1 | async-start | bytes 131072 | tf_op jit(solution)/shard_map/slice | solution.py:111
  202.2 1.8 copy-start.2
Sparse Core Ops, SparseCore 0:
  30.9 68.6 all-gather.1
where the time goes:
time: 216 us; the launch traced here: 214 us
  matrix products  125 us (58%)
  other arithmetic  24.2 us (11%)
  starting transfers between devices  18.1 us (8%)
  between operations  13.8 us (6%)
  blocking collectives  12.6 us (6%)
  waiting for transfers between devices  10.9 us (5%)
  local copies, waits for them, and re-layouts  8.52 us (4%)
    dot_general x16, matrix products, near_leaf(): jnp.einsum('kcn,knm->cm', source_charge, near_kernel, preferred_element_t...  69 us
    dot_general x16, matrix products, near_leaf(): jnp.dot(pick_table, flat_pair, preferred_element_type=jnp.float32)  31.3 us
    ppermute x5, starting transfers between devices, from_partner(): return lax.ppermute(block, axis, route)  14.7 us
    all_gather x1, blocking collectives, fetch_roots(): return lax.all_gather(group_root[None], 'narrow', axis=0, tiled=True)  12.6 us
    sub x16, other arithmetic, near_leaf(): leaf_ids - first_leaf  10.9 us
    ppermute x5, waiting for transfers between devices, from_partner(): return lax.ppermute(block, axis, route)  10.9 us
    reduce_sum x16, other arithmetic, near_leaf(): target_sq = jnp.sum(target_wide * target_wide, axis=0)  9.91 us
    dot_general x9, matrix products, merge_up(): jnp.einsum('mrt,mts->mrs', joined[:, :rhs_count], transfer.astype(jnp.flo...  5.79 us
  transfers between devices with their start and end apart: 8, of which 4 were waited for; matrix products, arithmetic and copies ran while one was open for 65% of the time, Pallas kernels for 0%

commit v1 on v0

v1 whole, which is shorter than its diff:
```python
import functools
import math

import jax
import jax.numpy as jnp
from jax import lax
from jax.experimental import pallas as pl
from jax.experimental.pallas import tpu as pltpu
from jax.sharding import PartitionSpec as P

F32 = jnp.float32
BF16 = jnp.bfloat16
MESH = pl.DeviceIdType.MESH
RATE = 1.5 * math.log2(math.e)
LAST_DIMS = (((1,), (1,)), ((), ()))
FIRST_DIMS = (((0,), (0,)), ((), ()))
VMEM_BYTES = 56 * 2**20


def dot(a, b, dims=(((1,), (0,)), ((), ()))):
    return lax.dot_general(a, b, dims, preferred_element_type=F32)


def split3(x):
    first = x.astype(BF16).astype(F32)
    rest = x - first
    second = rest.astype(BF16).astype(F32)
    return first, second, rest - second


def hi_lo(x):
    high = x.astype(BF16)
    return high, (x - high.astype(F32)).astype(BF16)


def tail_rows(parts, slots):
    row = lax.broadcasted_iota(jnp.int32, (8, parts[0].shape[1]), 0)
    ones = (row >= slots[1]) & (row < slots[1] + 3)
    rows = jnp.where(ones, 1.0, 0.0)
    for i, part in enumerate(parts):
        rows = jnp.where(row == slots[0] + i, part, rows)
    return rows


def source_rows(points):
    norm = -RATE * jnp.sum(points * points, axis=0, keepdims=True)
    return jnp.concatenate([*split3(2.0 * RATE * points), tail_rows(split3(norm), (0, 3))], axis=0)


def target_rows(points):
    norm = -RATE * jnp.sum(points * points, axis=0, keepdims=True)
    return jnp.concatenate([points, points, points, tail_rows(split3(norm), (3, 0))], axis=0)


def merge(left, right, transfer, chosen, rhs):
    skel = left.shape[1]
    joined = jnp.concatenate([left, right], axis=1)
    high, low = hi_lo(joined[:rhs])
    rows = jnp.concatenate([high, low, joined[rhs:].astype(BF16)], axis=0)
    index = lax.broadcasted_iota(jnp.int32, (2 * skel, skel), 0)
    table = jnp.where(index == chosen, 1.0, 0.0).astype(BF16)
    both = dot(rows, jnp.concatenate([transfer, table], axis=1))
    weight = both[:rhs, :skel] + both[rhs : 2 * rhs, :skel]
    return jnp.concatenate([weight, both[2 * rhs :, skel:]], axis=0)


def node_field(source, target, rhs):
    log_kernel = dot(
        source_rows(source[rhs:]).astype(BF16), target_rows(target).astype(BF16), FIRST_DIMS
    )
    kernel_high, kernel_low = hi_lo(jnp.exp2(log_kernel))
    high, low = hi_lo(source[:rhs])
    both = dot(jnp.concatenate([high, low], axis=0), kernel_high)
    return both[:rhs] + both[rhs:] + dot(high, kernel_low)


def times_transposed(field, matrix):
    rows = field.shape[0]
    both = dot(jnp.concatenate(hi_lo(field), axis=0), matrix, LAST_DIMS)
    return both[:rows] + both[rows:]


def up_kernel(
    points, charges, basis, leaf_skel, transfer, skel,
    node, own_near, points_low, points_high, charges_low, charges_high,
    nodes, sources, targets, kernel_a, kernel_b, send_sem, recv_sem,
):
    leaves, rhs, box = charges.shape
    skel_count = basis.shape[2]
    wide = lax.axis_size("wide")
    me = lax.axis_index("wide")
    right, left = lax.rem(me + 1, wide), lax.rem(me + wide - 1, wide)
    barrier = pltpu.get_barrier_semaphore()
    for other in (left, right):
        pl.semaphore_signal(barrier, inc=1, device_id={"wide": other}, device_id_type=MESH)
    pl.semaphore_wait(barrier, 2)
    copies = []
    for i, (src, dst, other) in enumerate(
        (
            (charges, charges_low, right),
            (charges, charges_high, left),
            (points, points_low, right),
            (points, points_high, left),
        )
    ):
        copies.append(
            pltpu.make_async_remote_copy(
                src_ref=src, dst_ref=dst, send_sem=send_sem.at[i], recv_sem=recv_sem.at[i],
                device_id={"wide": other}, device_id_type=MESH,
            )
        )
    for copy in copies:
        copy.start()

    step = 4

    def leaf_nodes(first, carry):
        for leaf in [first * step + i for i in range(step)]:
            spots = points[leaf]
            index = lax.broadcasted_iota(jnp.int32, (box, skel_count), 0)
            table = jnp.where(index == leaf_skel[pl.ds(leaf, 1), :], 1.0, 0.0).astype(BF16)
            weight = dot(charges[leaf], basis[leaf])
            coords = dot(spots, table)
            nodes[leaf] = jnp.concatenate([weight, coords], axis=0)
        return carry

    lax.fori_loop(0, leaves // step, leaf_nodes, 0)
    level = [nodes[leaf] for leaf in range(leaves)]
    while len(level) > 1:
        parents = len(level) // 2
        level = [
            merge(
                level[2 * p], level[2 * p + 1], transfer[parents - 1 + p],
                skel[parents - 1 + p : parents + p, :], rhs,
            )
            for p in range(parents)
        ]
    node[...] = level[0]

    def rows(leaf, carry):
        spots = points[leaf].astype(F32)
        sources[leaf] = source_rows(spots).T.astype(BF16)
        targets[leaf] = target_rows(spots).astype(BF16)
        return carry

    lax.fori_loop(0, leaves, rows, 0)

    def fill(leaf, buffer):
        buffer[...] = jnp.exp2(dot(sources[leaf], targets[leaf])).astype(BF16)

    fill(0, kernel_a)

    def two_leaves(pair, carry):
        fill(2 * pair + 1, kernel_b)
        own_near[2 * pair] = dot(charges[2 * pair], kernel_a[...])
        fill(lax.rem(2 * pair + 2, leaves), kernel_a)
        own_near[2 * pair + 1] = dot(charges[2 * pair + 1], kernel_b[...])
        return carry

    lax.fori_loop(0, leaves // 2, two_leaves, 0)
    for copy in copies:
        copy.wait()


def near_kernel(
    near_list, points_low, points, points_high, charges_low, charges, charges_high, own_near,
    near_out, near_charges, sources, targets, kernel_a, kernel_b, sem,
):
    leaves, _, box = points.shape
    near = near_list.shape[1]
    first_leaf = (lax.axis_index("wide") - 1) * leaves
    copies = [
        pltpu.make_async_copy(src, near_charges.at[pl.ds(i * leaves, leaves)], sem.at[i])
        for i, src in enumerate((charges_low, charges, charges_high))
    ]
    for copy in copies:
        copy.start()

    def rows(leaf, carry):
        for i, part in enumerate((points_low, points, points_high)):
            spots = part[leaf].astype(F32)
            sources[i * leaves + leaf] = source_rows(spots).T.astype(BF16)
            if i == 1:
                targets[leaf] = target_rows(spots).astype(BF16)
        return carry

    lax.fori_loop(0, leaves, rows, 0)
    for copy in copies:
        copy.wait()

    def fill(leaf, k, buffer):
        source = sources[near_list[leaf, k] - first_leaf]
        buffer[...] = jnp.exp2(dot(source, targets[leaf])).astype(BF16)

    fill(0, 1, kernel_a)

    def two_leaves(pair, carry):
        steps = [(2 * pair + i, k) for i in range(2) for k in range(1, near)]
        steps.append((lax.rem(2 * pair + 2, leaves), 1))
        total = None
        for i, (leaf, k) in enumerate(steps[:-1]):
            now, later = (kernel_a, kernel_b) if i % 2 == 0 else (kernel_b, kernel_a)
            fill(*steps[i + 1], later)
            part = dot(near_charges[near_list[leaf, k] - first_leaf], now[...])
            total = (own_near[leaf] if k == 1 else total) + part
            if k == near - 1:
                near_out[leaf] = total
        return carry

    lax.fori_loop(0, leaves // 2, two_leaves, 0)


def down_kernel(
    far_list, all_nodes, own_node, top_transfer, top_skel, transfer, basis, near_out,
    out, tree, roots, send_sem, recv_sem,
):
    leaves, rhs, box = near_out.shape
    skel_count = basis.shape[2]
    wide, groups = lax.axis_size("wide"), lax.axis_size("narrow")
    me, group = lax.axis_index("wide"), lax.axis_index("narrow")
    others = [lax.rem(group + d, groups) for d in range(1, groups)]
    barrier = pltpu.get_barrier_semaphore()
    for other in others:
        pl.semaphore_signal(barrier, inc=1, device_id={"narrow": other}, device_id_type=MESH)

    parents = wide // 2
    while parents >= 1:
        step = min(4, parents)
        base = parents - 1

        def level(first, carry, step=step, base=base, parents=parents):
            for p in [first * step + i for i in range(step)]:
                if parents == wide // 2:
                    left = all_nodes[2 * p * groups + group]
                    right = all_nodes[(2 * p + 1) * groups + group]
                else:
                    left, right = tree[2 * base + 1 + 2 * p], tree[2 * base + 2 + 2 * p]
                tree[base + p] = merge(
                    left, right, top_transfer[base + p], top_skel[pl.ds(base + p, 1), :], rhs
                )
            return carry

        if step == parents:
            level(0, 0)
        else:
            lax.fori_loop(0, parents // step, level, 0)
        parents //= 2

    pl.semaphore_wait(barrier, groups - 1)
    copies = [
        pltpu.make_async_remote_copy(
            src_ref=tree.at[0], dst_ref=roots.at[i], send_sem=send_sem.at[i],
            recv_sem=recv_sem.at[i], device_id={"narrow": other}, device_id_type=MESH,
        )
        for i, other in enumerate(others)
    ]
    for copy in copies:
        copy.start()
    target = own_node[...][rhs:]
    far = None
    for i in range(far_list.shape[1]):
        e = far_list[0, i]
        source = all_nodes[lax.rem(e, wide) * groups + lax.div(e, wide)]
        part = node_field(source, target, rhs)
        far = part if far is None else far + part
    for copy in copies:
        copy.wait()
    target = tree[0][rhs:]
    field = None
    for i in range(groups - 1):
        part = node_field(roots[i], target, rhs)
        field = part if field is None else field + part
    for section in reversed(range(wide.bit_length() - 1)):
        slot = (wide >> section + 1) - 1 + lax.div(me, 2 << section)
        side = lax.rem(lax.div(me, 1 << section), 2)
        start = pl.multiple_of(side * skel_count, skel_count)
        field = times_transposed(field, top_transfer[slot, pl.ds(start, skel_count), :])
    fields = [field + far]
    while len(fields) < leaves:
        parents = len(fields)
        both = [times_transposed(fields[p], transfer[parents - 1 + p]) for p in range(parents)]
        fields = [half for pair in both for half in (pair[:, :skel_count], pair[:, skel_count:])]
    scale = 1.0 / math.sqrt(box)
    for leaf in range(leaves):
        far_part = times_transposed(fields[leaf], basis[leaf])
        out[leaf] = ((near_out[leaf] + far_part) * scale).astype(BF16)


def shards(
    points, charges, leaf_interp_basis, leaf_skeleton, local_transfer, local_skeleton,
    top_transfer, top_skeleton, near_list, far_list,
):
    points, charges, basis = points[0], charges[0], leaf_interp_basis[0]
    leaves, dims, box = points.shape
    rhs, skel = charges.shape[1], basis.shape[2]
    groups, wide = lax.axis_size("narrow"), lax.axis_size("wide")
    near = near_list.shape[2]
    vmem = pl.BlockSpec(memory_space=pltpu.VMEM)
    smem = pl.BlockSpec(memory_space=pltpu.SMEM)
    anywhere = pl.BlockSpec(memory_space=pl.ANY)

    def shape(dtype, *dims):
        return jax.ShapeDtypeStruct(dims, dtype)

    def cost(blocks):
        return pl.CostEstimate(
            flops=blocks * 2 * box * box * 288, bytes_accessed=4 * 2**20,
            transcendentals=blocks * box * box,
        )

    kernel_pair = [pltpu.VMEM((box, box), BF16)] * 2
    node, own_near, points_low, points_high, charges_low, charges_high = pl.pallas_call(
        up_kernel,
        out_shape=(
            shape(F32, rhs + dims, skel), shape(F32, leaves, rhs, box),
            shape(BF16, *points.shape), shape(BF16, *points.shape),
            shape(BF16, *charges.shape), shape(BF16, *charges.shape),
        ),
        in_specs=[vmem] * 6,
        out_specs=(vmem, vmem, anywhere, anywhere, anywhere, anywhere),
        scratch_shapes=[
            pltpu.VMEM((leaves, rhs + dims, skel), F32),
            pltpu.VMEM((leaves, box, 32), BF16),
            pltpu.VMEM((leaves, 32, box), BF16),
            *kernel_pair,
            pltpu.SemaphoreType.DMA((4,)),
            pltpu.SemaphoreType.DMA((4,)),
        ],
        compiler_params=pltpu.CompilerParams(
            collective_id=0, has_side_effects=True, vmem_limit_bytes=VMEM_BYTES
        ),
        cost_estimate=cost(leaves),
        name="up",
    )(points, charges, basis, leaf_skeleton[0], local_transfer[0], local_skeleton[0])
    all_nodes = lax.all_gather(node[None], ("wide", "narrow"), axis=0, tiled=True)
    near_out = pl.pallas_call(
        near_kernel,
        out_shape=shape(F32, leaves, rhs, box),
        in_specs=[smem, vmem, vmem, vmem, anywhere, anywhere, anywhere, vmem],
        out_specs=vmem,
        scratch_shapes=[
            pltpu.VMEM((3 * leaves, rhs, box), BF16),
            pltpu.VMEM((3 * leaves, box, 32), BF16),
            pltpu.VMEM((leaves, 32, box), BF16),
            *kernel_pair,
            pltpu.SemaphoreType.DMA((3,)),
        ],
        compiler_params=pltpu.CompilerParams(vmem_limit_bytes=VMEM_BYTES),
        cost_estimate=cost(leaves * (near - 1)),
        name="near",
    )(
        near_list[0], points_low, points, points_high, charges_low, charges, charges_high, own_near
    )
    out = pl.pallas_call(
        down_kernel,
        out_shape=shape(BF16, leaves, rhs, box),
        in_specs=[smem] + [vmem] * 7,
        out_specs=vmem,
        scratch_shapes=[
            pltpu.VMEM((wide - 1, rhs + dims, skel), F32),
            pltpu.VMEM((groups - 1, rhs + dims, skel), F32),
            pltpu.SemaphoreType.DMA((groups - 1,)),
            pltpu.SemaphoreType.DMA((groups - 1,)),
        ],
        compiler_params=pltpu.CompilerParams(
            collective_id=1, has_side_effects=True, vmem_limit_bytes=VMEM_BYTES
        ),
        name="down",
    )(
        far_list[0], all_nodes, node, top_transfer[0], top_skeleton[0], local_transfer[0], basis,
        near_out,
    )
    return out[None]


def solution(mesh):
    return jax.shard_map(
        shards,
        mesh=mesh,
        in_specs=(
            P("narrow", "wide", None, None),
            P("narrow", "wide", None, None),
            P("narrow", "wide", None, None),
            P("narrow", "wide", None),
            P("narrow", "wide", None, None),
            P("narrow", "wide", None),
            P("narrow", None, None, None),
            P("narrow", None, None),
            P("narrow", "wide", None),
            P("narrow", "wide", None),
        ),
        out_specs=P("narrow", "wide", None, None),
        check_vma=False,
    )
```

time: 216 us -> 114 us (0.53)
  matrix products: 125 us -> 0 us
  Pallas kernels: 0 us -> 60.8 us
  other arithmetic: 24.2 us -> 0 us
  waiting for transfers between devices: 10.9 us -> 34.8 us
  starting transfers between devices: 18.1 us -> 0.01 us
  blocking collectives: 12.6 us -> 0 us
  local copies, waits for them, and re-layouts: 8.52 us -> 4.46 us
    dot_general x67 -> x0, matrix products: 125 us -> none  [the longest x16 69 us: near_leaf(): jnp.einsum('kcn,knm->cm', source_charge, near_kernel, preferred_element_t...]
    pallas_call x0 -> x3, Pallas kernels: none -> 60.8 us  [the longest x1 29.9 us: shards(): pl.pallas_call(near_kernel, out_shape=shape(F32, leaves, rhs, box), in_sp...]
    all_gather x1, waiting for transfers between devices: 0.02 us -> 34.7 us  [shards(): lax.all_gather(node[None], ('wide', 'narrow'), axis=0, tiled=True)]
    ppermute x7 -> x0, starting transfers between devices: 18.1 us -> none  [the longest x5 14.7 us: from_partner(): return lax.ppermute(block, axis, route)]
    all_gather x1 -> x0, blocking collectives: 12.6 us -> none  [fetch_roots(): return lax.all_gather(group_root[None], 'narrow', axis=0, tiled=True)]
    sub x16 -> x0, other arithmetic: 10.9 us -> none  [near_leaf(): leaf_ids - first_leaf]
    ppermute x7 -> x0, waiting for transfers between devices: 10.9 us -> none  [the longest x5 10.9 us: from_partner(): return lax.ppermute(block, axis, route)]
    reduce_sum x33 -> x0, other arithmetic: 10.2 us -> none  [the longest x16 9.91 us: near_leaf(): target_sq = jnp.sum(target_wide * target_wide, axis=0)]
  transfers between devices with their start and end apart: 8 -> 1, of which waited for: 4 -> 1; matrix products, arithmetic and copies ran while one was open for 65% -> 1% of each run, Pallas kernels for 0% -> 26%
where the time goes in v1:
time: 114 us; the launch traced here: 113 us
  Pallas kernels  60.8 us (53%)
  waiting for transfers between devices  34.8 us (31%)
  between operations  13.4 us (12%)
  local copies, waits for them, and re-layouts  4.46 us (4%)
    all_gather x1, waiting for transfers between devices, shards(): lax.all_gather(node[None], ('wide', 'narrow'), axis=0, tiled=True)  34.7 us
    pallas_call x1, Pallas kernels, shards(): pl.pallas_call(near_kernel, out_shape=shape(F32, leaves, rhs, box), in_sp...  29.9 us
    pallas_call x1, Pallas kernels, shards(): pl.pallas_call(up_kernel, out_shape=(shape(F32, rhs + dims, skel), shape(...  17.9 us
    pallas_call x1, Pallas kernels, shards(): pl.pallas_call(down_kernel, out_shape=shape(BF16, leaves, rhs, box), in_s...  13 us
    unnamed x7, local copies, waits for them, and re-layouts  3.79 us
  transfers between devices with their start and end apart: 1, of which 1 were waited for; matrix products, arithmetic and copies ran while one was open for 1% of the time, Pallas kernels for 26%

profile of v1, /device:TPU:0, one launch (start us, length us, event | category | flops | bytes accessed | tf_op | source)
XLA Modules:
  0.0 113.4 jit_solution(3935283578121607572)
XLA Ops:
  6.5 0.0 all-gather.3.cloned.1.call-start
  6.5 1.3 %copy.17 = s32[1,15,128]{2,1,0:T(8,128)} copy(s32[1,15,128]{2,0,1:T(1,128)} %param.15) | data formatting | bytes 15360
  7.8 0.0 copy-start.1
  7.8 0.0 copy-start
  7.8 17.9 %up.1 = (f32[40,128]{1,0:T(8,128)}, f32[16,32,512]{2,1,0:T(8,128)}, bf16[16,8,512]{2,1,0:T(8,128)(2,1)}, bf16[16,8,512]{2,1,0:T(8,128)(2,1)}, bf16[16,32,512]{2,...) custom-call(bf16[16,8,512]{2,1,0:T(8,128)(2,1)} %bitcast.29, bf16[16,32,512]{2,1,0:T(8,128)(2,1)} %bitcast.27, ...), custom_call_target="tpu_custom_call" | custom-call | flops 2415919104 | bytes 4194304 | tf_op jit(solution)/shard_map/up/pallas_call | solution.py:312
  25.8 0.0 all-gather.3.cloned.1.call-update
  25.8 0.0 copy-done.1
  25.8 0.7 copy.11.near_list
  26.5 0.0 copy-done
  26.5 0.6 copy.16
  27.1 29.9 %near.1.near_out = f32[16,32,512]{2,1,0:T(8,128)} custom-call(s32[16,8]{1,0:T(8,128)} %copy.11.near_list, bf16[16,8,512]{2,1,0:T(8,128)(2,1)} %get-tuple-element.12.points_low, bf16[16,8,512]{2,1,0:T(8,128)(2,1)} %bitcast.30, bf16[16,8,512]{2,1,0:T(8,128)(2,1)} %get-tuple-element.13.points_high, bf16[16,32,512]{2,1,0:T(8,128)(2,1)} %get-tuple-element.14.charges_low, ...), custom_call_target="tpu_custom_call" | custom-call | flops 16911433728 | bytes 4194304 | tf_op jit(solution)/shard_map/near/pallas_call | solution.py:336
  57.0 34.7 %all-gather.3.cloned.1.call-done = f32[5120,128]{1,0:T(8,128)} async-done(((f32[40,128]{1,0:T(8,128)}), f32[5120,128]{1,0:T(8,128)}) %all-gather.3.cloned.1.call-update) | async-done | bytes 2621456 | tf_op jit(solution)/shard_map/all_gather | solution.py:335
  91.7 13.0 %down.1 = bf16[16,32,512]{2,1,0:T(8,128)(2,1)} custom-call(s32[1,4]{1,0:T(1,128)} %bitcast.26, f32[128,40,128]{2,1,0:T(8,128)} %bitcast.16, f32[40,128]{1,0:T(8,128)} %get-tuple-element.11.own_node, bf16[31,256,128]{2,1,0:T(8,128)(2,1)} %bitcast.20, s32[31,128]{1,0:T(8,128)} %bitcast.23, bf16[15,256,128]{2,1,0:T(8,128)(2,1)} %bitcast.22, ...), custom_call_target="tpu_custom_call" | custom-call | tf_op jit(solution)/shard_map/down/pallas_call | solution.py:354
  104.7 1.9 %copy.19 = bf16[1,16,32,512]{3,2,1,0:T(8,128)(2,1)} copy(bf16[1,16,32,512]{3,2,1,0:T(8,128)(2,1)} %bitcast.17) | data formatting | bytes 1048576
Async XLA Ops:
  6.5 85.2 %all-gather.3.cloned.1.call-start = ((), (), s32[]{:S(2)}) async-start(), calls=%async_computation | async-start | bytes 2641920 | tf_op jit(solution)/shard_map/all_gather | solution.py:335
  7.8 18.0 %copy-start.1 = (s32[1,16,8]{1,2,0:T(8,128)S(1)}, s32[1,16,8]{1,2,0:T(8,128)}, u32[]{:S(2)}) copy-start(s32[1,16,8]{1,2,0:T(8,128)} %param.18) | copy-start | bytes 1540
  7.8 18.7 %copy-start = (s32[1,31,128]{2,0,1:T(1,128)S(1)}, s32[1,31,128]{2,0,1:T(1,128)}, u32[]{:S(2)}) copy-start(s32[1,31,128]{2,0,1:T(1,128)} %param.17) | copy-start | bytes 47620
Sparse Core Ops, SparseCore 0:
  25.9 65.7 all-gather.2

commit v2 on v1

v2 whole, which is shorter than its diff:
```python
import functools
import math

import jax
import jax.numpy as jnp
from jax import lax
from jax.experimental import pallas as pl
from jax.experimental.pallas import tpu as pltpu
from jax.sharding import PartitionSpec as P

F32 = jnp.float32
BF16 = jnp.bfloat16
MESH = pl.DeviceIdType.MESH
RATE = 1.5 * math.log2(math.e)
LAST_DIMS = (((1,), (1,)), ((), ()))
FIRST_DIMS = (((0,), (0,)), ((), ()))
VMEM_BYTES = 56 * 2**20


def dot(a, b, dims=(((1,), (0,)), ((), ()))):
    return lax.dot_general(a, b, dims, preferred_element_type=F32)


def split3(x):
    first = x.astype(BF16).astype(F32)
    rest = x - first
    second = rest.astype(BF16).astype(F32)
    return first, second, rest - second


def hi_lo(x):
    high = x.astype(BF16)
    return high, (x - high.astype(F32)).astype(BF16)


def tail_rows(parts, slots):
    row = lax.broadcasted_iota(jnp.int32, (8, parts[0].shape[1]), 0)
    ones = (row >= slots[1]) & (row < slots[1] + 3)
    rows = jnp.where(ones, 1.0, 0.0)
    for i, part in enumerate(parts):
        rows = jnp.where(row == slots[0] + i, part, rows)
    return rows


def source_rows(points):
    norm = -RATE * jnp.sum(points * points, axis=0, keepdims=True)
    return jnp.concatenate([*split3(2.0 * RATE * points), tail_rows(split3(norm), (0, 3))], axis=0)


def target_rows(points):
    norm = -RATE * jnp.sum(points * points, axis=0, keepdims=True)
    return jnp.concatenate([points, points, points, tail_rows(split3(norm), (3, 0))], axis=0)


def merge(left, right, transfer, chosen, rhs):
    skel = left.shape[1]
    joined = jnp.concatenate([left, right], axis=1)
    high, low = hi_lo(joined[:rhs])
    rows = jnp.concatenate([high, low, joined[rhs:].astype(BF16)], axis=0)
    index = lax.broadcasted_iota(jnp.int32, (2 * skel, skel), 0)
    table = jnp.where(index == chosen, 1.0, 0.0).astype(BF16)
    both = dot(rows, jnp.concatenate([transfer, table], axis=1))
    weight = both[:rhs, :skel] + both[rhs : 2 * rhs, :skel]
    return jnp.concatenate([weight, both[2 * rhs :, skel:]], axis=0)


def node_field(source, target, rhs):
    log_kernel = dot(
        source_rows(source[rhs:]).astype(BF16), target_rows(target).astype(BF16), FIRST_DIMS
    )
    kernel_high, kernel_low = hi_lo(jnp.exp2(log_kernel))
    high, low = hi_lo(source[:rhs])
    both = dot(jnp.concatenate([high, low], axis=0), kernel_high)
    return both[:rhs] + both[rhs:] + dot(high, kernel_low)


def times_transposed(field, matrix):
    rows = field.shape[0]
    both = dot(jnp.concatenate(hi_lo(field), axis=0), matrix, LAST_DIMS)
    return both[:rows] + both[rows:]


def main_kernel(
    near_list, far_list, points, charges, basis, transfer, top_transfer, leaf_skel, skel, top_skel,
    field_out, near_out,
    near_points, near_charges, basis_here, transfer_here, top_here, nodes, all_nodes, tree, roots,
    sources, targets, kernel_a, kernel_b, local_sem, send_sem, recv_sem,
):
    leaves, rhs, box = charges.shape
    skel_count = basis.shape[2]
    near = near_list.shape[0]
    wide, groups = lax.axis_size("wide"), lax.axis_size("narrow")
    me, group = lax.axis_index("wide"), lax.axis_index("narrow")
    chips = wide // 2
    side = math.isqrt(chips)
    core, chip = lax.rem(me, 2), lax.div(me, 2)
    row, column = lax.div(chip, side), lax.rem(chip, side)
    right, left = lax.rem(me + 1, wide), lax.rem(me + wide - 1, wide)
    sibling = chip * 2 + 1 - core

    def in_row(step):
        return lax.rem(column + step, side)

    def in_column(step):
        return lax.rem(row + step, side)

    def in_groups(step):
        return lax.rem(group + step, groups)

    row_peers = [(row * side + in_row(d)) * 2 + core for d in range(1, side)]
    column_peers = [(in_column(d) * side + column) * 2 + core for d in range(1, side)]
    group_peers = [in_groups(d) for d in range(1, groups)]

    local = [
        pltpu.make_async_copy(src, dst, local_sem.at[i])
        for i, (src, dst) in enumerate(
            (
                (charges, near_charges.at[pl.ds(leaves, leaves)]),
                (points, near_points.at[1]),
                (basis, basis_here),
                (transfer, transfer_here),
                (top_transfer, top_here),
            )
        )
    ]
    for copy in local:
        copy.start()
    barrier = pltpu.get_barrier_semaphore()
    wide_peers = [right, left] + row_peers + column_peers
    for other in wide_peers:
        pl.semaphore_signal(barrier, inc=1, device_id={"wide": other}, device_id_type=MESH)
    for other in group_peers:
        pl.semaphore_signal(barrier, inc=1, device_id={"narrow": other}, device_id_type=MESH)
    pl.semaphore_wait(barrier, len(wide_peers) + len(group_peers))

    used = []

    def exchange(src, dst, device, incoming=None):
        i = len(used)
        used.append(i)
        sems = {"send_sem": send_sem.at[i], "recv_sem": recv_sem.at[i]}
        sent = pltpu.make_async_remote_copy(
            src_ref=src, dst_ref=dst, device_id=device, device_id_type=MESH, **sems
        )
        landed = dst if incoming is None else incoming
        got = pltpu.make_async_remote_copy(
            src_ref=landed, dst_ref=landed, device_id=device, device_id_type=MESH, **sems
        )
        sent.start()
        return sent, got

    def finish(pairs):
        for sent, got in pairs:
            sent.wait_send()
            got.wait_recv()

    halo = []
    for other, block, place in ((right, 0, 0), (left, 2, 2 * leaves)):
        halo.append(
            exchange(charges, near_charges.at[pl.ds(place, leaves)], {"wide": other})
        )
        halo.append(exchange(points, near_points.at[block], {"wide": other}))

    for copy in local[:3]:
        copy.wait()
    step = 4

    def leaf_nodes(first, carry):
        for leaf in [first * step + i for i in range(step)]:
            spots = near_points[1, leaf]
            index = lax.broadcasted_iota(jnp.int32, (box, skel_count), 0)
            table = jnp.where(index == leaf_skel[pl.ds(leaf, 1), :], 1.0, 0.0).astype(BF16)
            weight = dot(near_charges[leaves + leaf], basis_here[leaf])
            coords = dot(spots, table)
            nodes[leaf] = jnp.concatenate([weight, coords], axis=0)
        return carry

    lax.fori_loop(0, leaves // step, leaf_nodes, 0)
    local[3].wait()
    level = [nodes[leaf] for leaf in range(leaves)]
    while len(level) > 1:
        parents = len(level) // 2
        level = [
            merge(
                level[2 * p], level[2 * p + 1], transfer_here[parents - 1 + p],
                skel[parents - 1 + p], rhs,
            )
            for p in range(parents)
        ]
    half = core * chips
    slot = half + chip
    all_nodes[group, slot] = level[0]
    mine = all_nodes.at[group, slot]
    stage_a = [
        exchange(
            mine, mine, {"wide": other},
            all_nodes.at[group, half + row * side + in_row(side - d)],
        )
        for d, other in enumerate(row_peers, 1)
    ]

    def own_rows(leaf, carry):
        spots = near_points[1, leaf].astype(F32)
        sources[leaves + leaf] = source_rows(spots).T.astype(BF16)
        targets[leaf] = target_rows(spots).astype(BF16)
        return carry

    lax.fori_loop(0, leaves, own_rows, 0)

    def fill_own(leaf, buffer):
        buffer[...] = jnp.exp2(dot(sources[leaves + leaf], targets[leaf])).astype(BF16)

    def own_pair(pair, carry):
        fill_own(2 * pair + 1, kernel_b)
        near_out[2 * pair] = dot(near_charges[leaves + 2 * pair], kernel_a[...])
        fill_own(lax.rem(2 * pair + 2, leaves), kernel_a)
        near_out[2 * pair + 1] = dot(near_charges[leaves + 2 * pair + 1], kernel_b[...])
        return carry

    fill_own(0, kernel_a)
    lax.fori_loop(0, leaves // 4, own_pair, 0)
    finish(stage_a)
    line = all_nodes.at[group, pl.ds(half + row * side, side)]
    stage_b = [
        exchange(
            line, line, {"wide": other},
            all_nodes.at[group, pl.ds(half + in_column(side - d) * side, side)],
        )
        for d, other in enumerate(column_peers, 1)
    ]
    lax.fori_loop(leaves // 4, leaves // 2, own_pair, 0)
    finish(stage_b)
    plane = all_nodes.at[group, pl.ds(half, chips)]
    other_half = pl.ds((1 - core) * chips, chips)
    stage_d = [
        exchange(
            plane, plane, {"narrow": other},
            all_nodes.at[in_groups(groups - d), pl.ds(half, chips)],
        )
        for d, other in enumerate(group_peers, 1)
    ]
    stage_c = [exchange(plane, plane, {"wide": sibling}, all_nodes.at[group, other_half])]
    finish(halo)

    def halo_rows(leaf, carry):
        for block in (0, 2):
            spots = near_points[block, leaf].astype(F32)
            sources[block * leaves + leaf] = source_rows(spots).T.astype(BF16)
        return carry

    lax.fori_loop(0, leaves, halo_rows, 0)
    first_leaf = (me - 1) * leaves

    def place_of(leaf, k):
        return jnp.clip(near_list[k, leaf] - first_leaf, 0, 3 * leaves - 1)

    def fill(leaf, k, buffer):
        source = sources[place_of(leaf, k)]
        buffer[...] = jnp.exp2(dot(source, targets[leaf])).astype(BF16)

    def two_leaves(pair, carry):
        steps = [(2 * pair + i, k) for i in range(2) for k in range(1, near)]
        steps.append((lax.rem(2 * pair + 2, leaves), 1))
        total = None
        for i, (leaf, k) in enumerate(steps[:-1]):
            now, later = (kernel_a, kernel_b) if i % 2 == 0 else (kernel_b, kernel_a)
            fill(*steps[i + 1], later)
            part = dot(near_charges[place_of(leaf, k)], now[...])
            total = (near_out[leaf] if k == 1 else total) + part
            if k == near - 1:
                near_out[leaf] = total
        return carry

    fill(0, 1, kernel_a)
    lax.fori_loop(0, 2, two_leaves, 0)
    finish(stage_c)
    local[4].wait()

    parents = chips
    while parents >= 1:
        step = min(4, parents)
        base = parents - 1

        def level(first, carry, step=step, base=base, parents=parents):
            for p in [first * step + i for i in range(step)]:
                if parents == chips:
                    left, right = all_nodes[group, p], all_nodes[group, chips + p]
                else:
                    left, right = tree[2 * base + 1 + 2 * p], tree[2 * base + 2 + 2 * p]
                tree[base + p] = merge(left, right, top_here[base + p], top_skel[base + p], rhs)
            return carry

        if step == parents:
            level(0, 0)
        else:
            lax.fori_loop(0, parents // step, level, 0)
        parents //= 2
    stage_r = [
        exchange(tree.at[0], roots.at[d], {"narrow": other}) for d, other in enumerate(group_peers)
    ]
    lax.fori_loop(2, 5, two_leaves, 0)
    finish(stage_d)
    stage_e = []
    for d in range(1, groups):
        other = in_groups(d)
        block = all_nodes.at[other, pl.ds(half, chips)]
        stage_e.append(
            exchange(block, block, {"wide": sibling}, all_nodes.at[other, other_half])
        )
    finish(stage_r)
    target = tree[0][rhs:]
    field = None
    for i in range(groups - 1):
        part = node_field(roots[i], target, rhs)
        field = part if field is None else field + part
    for section in reversed(range(wide.bit_length() - 1)):
        place = (wide >> section + 1) - 1 + lax.div(me, 2 << section)
        start = lax.rem(lax.div(me, 1 << section), 2) * skel_count
        matrix = top_here[place, pl.ds(pl.multiple_of(start, skel_count), skel_count), :]
        field = times_transposed(field, matrix)
    field_out[...] = field
    lax.fori_loop(5, leaves // 2, two_leaves, 0)
    finish(stage_e)
    target = all_nodes[group, slot][rhs:]
    field = field_out[...]
    for i in range(far_list.shape[1]):
        e = far_list[0, i]
        place = lax.rem(e, wide)
        source = all_nodes[lax.div(e, wide), lax.rem(place, 2) * chips + lax.div(place, 2)]
        field = field + node_field(source, target, rhs)
    field_out[...] = field


def down_kernel(field, transfer, basis, near_out, out):
    leaves, rhs, box = near_out.shape
    skel_count = basis.shape[2]
    fields = [field[...]]
    while len(fields) < leaves:
        parents = len(fields)
        both = [times_transposed(fields[p], transfer[parents - 1 + p]) for p in range(parents)]
        fields = [half for pair in both for half in (pair[:, :skel_count], pair[:, skel_count:])]
    scale = 1.0 / math.sqrt(box)
    for leaf in range(leaves):
        far_part = times_transposed(fields[leaf], basis[leaf])
        out[leaf] = ((near_out[leaf] + far_part) * scale).astype(BF16)


def shards(
    points, charges, leaf_interp_basis, leaf_skeleton, local_transfer, local_skeleton,
    top_transfer, top_skeleton, near_list, far_list,
):
    points, charges, basis = points[0], charges[0], leaf_interp_basis[0]
    leaves, dims, box = points.shape
    rhs, skel = charges.shape[1], basis.shape[2]
    groups, wide = lax.axis_size("narrow"), lax.axis_size("wide")
    vmem = pl.BlockSpec(memory_space=pltpu.VMEM)
    smem = pl.BlockSpec(memory_space=pltpu.SMEM)
    anywhere = pl.BlockSpec(memory_space=pl.ANY)

    def shape(dtype, *dims):
        return jax.ShapeDtypeStruct(dims, dtype)

    size = (rhs + dims, skel)
    side = math.isqrt(wide // 2)
    copies = 4 + 2 * (side - 1) + 1 + 3 * (groups - 1)
    field, near_out = pl.pallas_call(
        main_kernel,
        out_shape=(shape(F32, rhs, skel), shape(F32, leaves, rhs, box)),
        in_specs=[smem] * 2 + [anywhere] * 5 + [vmem] * 3,
        out_specs=(vmem, vmem),
        scratch_shapes=[
            pltpu.VMEM((3, *points.shape), BF16),
            pltpu.VMEM((3 * leaves, rhs, box), BF16),
            pltpu.VMEM(basis.shape, BF16),
            pltpu.VMEM(local_transfer.shape[1:], BF16),
            pltpu.VMEM(top_transfer.shape[1:], BF16),
            pltpu.VMEM((leaves, *size), F32),
            pltpu.VMEM((groups, wide, *size), F32),
            pltpu.VMEM((wide - 1, *size), F32),
            pltpu.VMEM((groups - 1, *size), F32),
            pltpu.VMEM((3 * leaves, box, 32), BF16),
            pltpu.VMEM((leaves, 32, box), BF16),
            pltpu.VMEM((box, box), BF16),
            pltpu.VMEM((box, box), BF16),
            pltpu.SemaphoreType.DMA((5,)),
            pltpu.SemaphoreType.DMA((copies,)),
            pltpu.SemaphoreType.DMA((copies,)),
        ],
        compiler_params=pltpu.CompilerParams(
            collective_id=0, has_side_effects=True, vmem_limit_bytes=VMEM_BYTES
        ),
        name="main",
    )(
        near_list[0].T, far_list[0], points, charges, basis, local_transfer[0], top_transfer[0],
        leaf_skeleton[0], jnp.swapaxes(local_skeleton, 0, 1), jnp.swapaxes(top_skeleton, 0, 1),
    )
    out = pl.pallas_call(
        down_kernel,
        out_shape=shape(BF16, leaves, rhs, box),
        in_specs=[vmem] * 4,
        out_specs=vmem,
        compiler_params=pltpu.CompilerParams(vmem_limit_bytes=VMEM_BYTES),
        name="down",
    )(field, local_transfer[0], basis, near_out)
    return out[None]


def solution(mesh):
    return jax.shard_map(
        shards,
        mesh=mesh,
        in_specs=(
            P("narrow", "wide", None, None),
            P("narrow", "wide", None, None),
            P("narrow", "wide", None, None),
            P("narrow", "wide", None),
            P("narrow", "wide", None, None),
            P("narrow", "wide", None),
            P("narrow", None, None, None),
            P("narrow", None, None),
            P("narrow", "wide", None),
            P("narrow", "wide", None),
        ),
        out_specs=P("narrow", "wide", None, None),
        check_vma=False,
    )
```

time: 114 us -> 61.8 us (0.54)
  waiting for transfers between devices: 34.8 us -> 0 us
  between operations: 13.4 us -> 0.01 us
  local copies, waits for them, and re-layouts: 4.46 us -> 0 us
    all_gather x1 -> x0, waiting for transfers between devices: 34.7 us -> none  [shards(): lax.all_gather(node[None], ('wide', 'narrow'), axis=0, tiled=True)]
    pallas_call x2 -> x1, Pallas kernels: 47.8 us -> 56.9 us  [shards(): pl.pallas_call(main_kernel, out_shape=(shape(F32, rhs, skel), shape(F32,...]
    pallas_call x1, Pallas kernels: 13 us -> 4.39 us  [shards(): pl.pallas_call(down_kernel, out_shape=shape(BF16, leaves, rhs, box), in_s...]
    unnamed x7 -> x0, local copies, waits for them, and re-layouts: 3.79 us -> none
  transfers between devices with their start and end apart: 1 -> 0, of which waited for: 1 -> 0; matrix products, arithmetic and copies ran while one was open for 1% -> 0% of each run, Pallas kernels for 26% -> 0%
where the time goes in v2:
time: 61.8 us; the launch traced here: 61.3 us
  Pallas kernels  61.3 us (99%)
    pallas_call x1, Pallas kernels, shards(): pl.pallas_call(main_kernel, out_shape=(shape(F32, rhs, skel), shape(F32,...  56.9 us
    pallas_call x1, Pallas kernels, shards(): pl.pallas_call(down_kernel, out_shape=shape(BF16, leaves, rhs, box), in_s...  4.39 us

profile of v2, /device:TPU:0, one launch (start us, length us, event | category | flops | bytes accessed | tf_op | source)
XLA Modules:
  0.0 61.3 jit_solution(4003545541622462615)
XLA Ops:
  0.0 56.9 %main.1 = (f32[32,128]{1,0:T(8,128)}, f32[16,32,512]{2,1,0:T(8,128)}) custom-call(s32[8,16]{1,0:T(8,128)} %bitcast.23, s32[1,4]{1,0:T(1,128)} %bitcast.24, bf16[16,8,512]{2,1,0:T(8,128)(2,1)} %bitcast.19, bf16[16,32,512]{2,1,0:T(8,128)(2,1)} %bitcast.18, bf16[16,512,128]{2,1,0:T(8,128)(2,1)} %bitcast.13, bf16[15,256,128]{2,1,0:T(8,128)(2,1)} %bitcast.15, ...), custom_call_target="tpu_custom_call" | custom-call | tf_op jit(solution)/shard_map/main/pallas_call | solution.py:366
  56.9 4.4 %down.1 = bf16[16,32,512]{2,1,0:T(8,128)(2,1)} custom-call(f32[32,128]{1,0:T(8,128)} %get-tuple-element.7.field, bf16[15,256,128]{2,1,0:T(8,128)(2,1)} %bitcast.16, bf16[16,512,128]{2,1,0:T(8,128)(2,1)} %bitcast.14, f32[16,32,512]{2,1,0:T(8,128)} %get-tuple-element.8.near_out), custom_call_target="tpu_custom_call" | custom-call | tf_op jit(solution)/shard_map/down/pallas_call | solution.py:397

commit v3 on v2

--- a/solution.py
+++ b/solution.py
@@ -154,12 +154,12 @@
             sent.wait_send()
             got.wait_recv()
 
-    halo = []
-    for other, block, place in ((right, 0, 0), (left, 2, 2 * leaves)):
-        halo.append(
-            exchange(charges, near_charges.at[pl.ds(place, leaves)], {"wide": other})
-        )
-        halo.append(exchange(points, near_points.at[block], {"wide": other}))
+    sides = ((right, 0), (left, 2))
+    halo_points = [exchange(points, near_points.at[b], {"wide": other}) for other, b in sides]
+    halo_charges = [
+        exchange(charges, near_charges.at[pl.ds(b * leaves, leaves)], {"wide": other})
+        for other, b in sides
+    ]
 
     for copy in local[:3]:
         copy.wait()
@@ -199,26 +199,28 @@
         for d, other in enumerate(row_peers, 1)
     ]
 
-    def own_rows(leaf, carry):
+    finish(halo_points)
+
+    def fill_own(leaf, buffer):
         spots = near_points[1, leaf].astype(F32)
-        sources[leaves + leaf] = source_rows(spots).T.astype(BF16)
-        targets[leaf] = target_rows(spots).astype(BF16)
+        source = source_rows(spots).T.astype(BF16)
+        target = target_rows(spots).astype(BF16)
+        sources[leaves + leaf] = source
+        targets[leaf] = target
+        buffer[...] = jnp.exp2(dot(source, target)).astype(BF16)
+
+    def own_pair(pair, carry):
+        for i, (now, later) in enumerate(((kernel_a, kernel_b), (kernel_b, kernel_a))):
+            leaf = 2 * pair + i
+            fill_own(lax.rem(leaf + 1, leaves), later)
+            near_out[leaf] = dot(near_charges[leaves + leaf], now[...])
+            for block in (0, 2):
+                spots = near_points[block, leaf].astype(F32)
+                sources[block * leaves + leaf] = source_rows(spots).T.astype(BF16)
         return carry
 
-    lax.fori_loop(0, leaves, own_rows, 0)
-
-    def fill_own(leaf, buffer):
-        buffer[...] = jnp.exp2(dot(sources[leaves + leaf], targets[leaf])).astype(BF16)
-
-    def own_pair(pair, carry):
-        fill_own(2 * pair + 1, kernel_b)
-        near_out[2 * pair] = dot(near_charges[leaves + 2 * pair], kernel_a[...])
-        fill_own(lax.rem(2 * pair + 2, leaves), kernel_a)
-        near_out[2 * pair + 1] = dot(near_charges[leaves + 2 * pair + 1], kernel_b[...])
-        return carry
-
     fill_own(0, kernel_a)
-    lax.fori_loop(0, leaves // 4, own_pair, 0)
+    lax.fori_loop(0, leaves // 2, own_pair, 0)
     finish(stage_a)
     line = all_nodes.at[group, pl.ds(half + row * side, side)]
     stage_b = [
@@ -228,27 +230,7 @@
         )
         for d, other in enumerate(column_peers, 1)
     ]
-    lax.fori_loop(leaves // 4, leaves // 2, own_pair, 0)
-    finish(stage_b)
-    plane = all_nodes.at[group, pl.ds(half, chips)]
-    other_half = pl.ds((1 - core) * chips, chips)
-    stage_d = [
-        exchange(
-            plane, plane, {"narrow": other},
-            all_nodes.at[in_groups(groups - d), pl.ds(half, chips)],
-        )
-        for d, other in enumerate(group_peers, 1)
-    ]
-    stage_c = [exchange(plane, plane, {"wide": sibling}, all_nodes.at[group, other_half])]
-    finish(halo)
-
-    def halo_rows(leaf, carry):
-        for block in (0, 2):
-            spots = near_points[block, leaf].astype(F32)
-            sources[block * leaves + leaf] = source_rows(spots).T.astype(BF16)
-        return carry
-
-    lax.fori_loop(0, leaves, halo_rows, 0)
+    finish(halo_charges)
     first_leaf = (me - 1) * leaves
 
     def place_of(leaf, k):
@@ -272,7 +254,19 @@
         return carry
 
     fill(0, 1, kernel_a)
-    lax.fori_loop(0, 2, two_leaves, 0)
+    lax.fori_loop(0, 1, two_leaves, 0)
+    finish(stage_b)
+    plane = all_nodes.at[group, pl.ds(half, chips)]
+    other_half = pl.ds((1 - core) * chips, chips)
+    stage_d = [
+        exchange(
+            plane, plane, {"narrow": other},
+            all_nodes.at[in_groups(groups - d), pl.ds(half, chips)],
+        )
+        for d, other in enumerate(group_peers, 1)
+    ]
+    stage_c = [exchange(plane, plane, {"wide": sibling}, all_nodes.at[group, other_half])]
+    lax.fori_loop(1, 3, two_leaves, 0)
     finish(stage_c)
     local[4].wait()
 
@@ -298,7 +292,7 @@
     stage_r = [
         exchange(tree.at[0], roots.at[d], {"narrow": other}) for d, other in enumerate(group_peers)
     ]
-    lax.fori_loop(2, 5, two_leaves, 0)
+    lax.fori_loop(3, 6, two_leaves, 0)
     finish(stage_d)
     stage_e = []
     for d in range(1, groups):
@@ -319,7 +313,7 @@
         matrix = top_here[place, pl.ds(pl.multiple_of(start, skel_count), skel_count), :]
         field = times_transposed(field, matrix)
     field_out[...] = field
-    lax.fori_loop(5, leaves // 2, two_leaves, 0)
+    lax.fori_loop(6, leaves // 2, two_leaves, 0)
     finish(stage_e)
     target = all_nodes[group, slot][rhs:]
     field = field_out[...]
@@ -331,18 +325,31 @@
     field_out[...] = field
 
 
-def down_kernel(field, transfer, basis, near_out, out):
+def down_kernel(
+    field, transfer, basis, near_out, out, transfer_here, basis_here, near_here, sem
+):
     leaves, rhs, box = near_out.shape
     skel_count = basis.shape[2]
+    copies = [
+        pltpu.make_async_copy(src, dst, sem.at[i])
+        for i, (src, dst) in enumerate(
+            ((transfer, transfer_here), (basis, basis_here), (near_out, near_here))
+        )
+    ]
+    for copy in copies:
+        copy.start()
+    copies[0].wait()
     fields = [field[...]]
     while len(fields) < leaves:
         parents = len(fields)
-        both = [times_transposed(fields[p], transfer[parents - 1 + p]) for p in range(parents)]
+        both = [times_transposed(fields[p], transfer_here[parents - 1 + p]) for p in range(parents)]
         fields = [half for pair in both for half in (pair[:, :skel_count], pair[:, skel_count:])]
+    copies[1].wait()
+    copies[2].wait()
     scale = 1.0 / math.sqrt(box)
     for leaf in range(leaves):
-        far_part = times_transposed(fields[leaf], basis[leaf])
-        out[leaf] = ((near_out[leaf] + far_part) * scale).astype(BF16)
+        far_part = times_transposed(fields[leaf], basis_here[leaf])
+        out[leaf] = ((near_here[leaf] + far_part) * scale).astype(BF16)
 
 
 def shards(
@@ -397,8 +404,14 @@
     out = pl.pallas_call(
         down_kernel,
         out_shape=shape(BF16, leaves, rhs, box),
-        in_specs=[vmem] * 4,
+        in_specs=[vmem] + [anywhere] * 3,
         out_specs=vmem,
+        scratch_shapes=[
+            pltpu.VMEM(local_transfer.shape[1:], BF16),
+            pltpu.VMEM(basis.shape, BF16),
+            pltpu.VMEM((leaves, rhs, box), F32),
+            pltpu.SemaphoreType.DMA((3,)),
+        ],
         compiler_params=pltpu.CompilerParams(vmem_limit_bytes=VMEM_BYTES),
         name="down",
     )(field, local_transfer[0], basis, near_out)

time: 61.8 us -> 56.3 us (0.911)
  Pallas kernels: 61.3 us -> 55.7 us
    pallas_call x1, Pallas kernels: 56.9 us -> 51.2 us  [shards(): pl.pallas_call(main_kernel, out_shape=(shape(F32, rhs, skel), shape(F32,...]
where the time goes in v3:
time: 56.3 us; the launch traced here: 55.7 us
  Pallas kernels  55.7 us (99%)
    pallas_call x1, Pallas kernels, shards(): pl.pallas_call(main_kernel, out_shape=(shape(F32, rhs, skel), shape(F32,...  51.2 us
    pallas_call x1, Pallas kernels, shards(): pl.pallas_call(down_kernel, out_shape=shape(BF16, leaves, rhs, box), in_s...  4.56 us

profile of v3, /device:TPU:0, one launch (start us, length us, event | category | flops | bytes accessed | tf_op | source)
XLA Modules:
  0.0 55.7 jit_solution(16971577519796477091)
XLA Ops:
  0.0 51.2 %main.1 = (f32[32,128]{1,0:T(8,128)}, f32[16,32,512]{2,1,0:T(8,128)}) custom-call(s32[8,16]{1,0:T(8,128)} %bitcast.23, s32[1,4]{1,0:T(1,128)} %bitcast.24, bf16[16,8,512]{2,1,0:T(8,128)(2,1)} %bitcast.19, bf16[16,32,512]{2,1,0:T(8,128)(2,1)} %bitcast.18, bf16[16,512,128]{2,1,0:T(8,128)(2,1)} %bitcast.13, bf16[15,256,128]{2,1,0:T(8,128)(2,1)} %bitcast.15, ...), custom_call_target="tpu_custom_call" | custom-call | tf_op jit(solution)/shard_map/main/pallas_call | solution.py:373
  51.2 4.6 %down.1 = bf16[16,32,512]{2,1,0:T(8,128)(2,1)} custom-call(f32[32,128]{1,0:T(8,128)} %get-tuple-element.7.field, bf16[15,256,128]{2,1,0:T(8,128)(2,1)} %bitcast.16, bf16[16,512,128]{2,1,0:T(8,128)(2,1)} %bitcast.14, f32[16,32,512]{2,1,0:T(8,128)} %get-tuple-element.8.near_out), custom_call_target="tpu_custom_call" | custom-call | tf_op jit(solution)/shard_map/down/pallas_call | solution.py:404

commit v4 on v3

--- a/solution.py
+++ b/solution.py
@@ -82,8 +82,8 @@
 
 def main_kernel(
     near_list, far_list, points, charges, basis, transfer, top_transfer, leaf_skel, skel, top_skel,
-    field_out, near_out,
-    near_points, near_charges, basis_here, transfer_here, top_here, nodes, all_nodes, tree, roots,
+    out,
+    near_out, near_points, near_charges, basis_here, transfer_here, top_here, nodes, all_nodes, tree, roots, top_field,
     sources, targets, kernel_a, kernel_b, local_sem, send_sem, recv_sem,
 ):
     leaves, rhs, box = charges.shape
@@ -199,7 +199,6 @@
         for d, other in enumerate(row_peers, 1)
     ]
 
-    finish(halo_points)
 
     def fill_own(leaf, buffer):
         spots = near_points[1, leaf].astype(F32)
@@ -214,13 +213,20 @@
             leaf = 2 * pair + i
             fill_own(lax.rem(leaf + 1, leaves), later)
             near_out[leaf] = dot(near_charges[leaves + leaf], now[...])
+        return carry
+
+    def own_pair_and_halo(pair, carry):
+        own_pair(pair, carry)
+        for leaf in [(pair - leaves // 4) * 4 + i for i in range(4)]:
             for block in (0, 2):
                 spots = near_points[block, leaf].astype(F32)
                 sources[block * leaves + leaf] = source_rows(spots).T.astype(BF16)
         return carry
 
     fill_own(0, kernel_a)
-    lax.fori_loop(0, leaves // 2, own_pair, 0)
+    lax.fori_loop(0, leaves // 4, own_pair, 0)
+    finish(halo_points)
+    lax.fori_loop(leaves // 4, 3 * leaves // 8, own_pair_and_halo, 0)
     finish(stage_a)
     line = all_nodes.at[group, pl.ds(half + row * side, side)]
     stage_b = [
@@ -230,6 +236,7 @@
         )
         for d, other in enumerate(column_peers, 1)
     ]
+    lax.fori_loop(3 * leaves // 8, leaves // 2, own_pair_and_halo, 0)
     finish(halo_charges)
     first_leaf = (me - 1) * leaves
 
@@ -254,7 +261,7 @@
         return carry
 
     fill(0, 1, kernel_a)
-    lax.fori_loop(0, 1, two_leaves, 0)
+    lax.fori_loop(0, 2, two_leaves, 0)
     finish(stage_b)
     plane = all_nodes.at[group, pl.ds(half, chips)]
     other_half = pl.ds((1 - core) * chips, chips)
@@ -266,7 +273,7 @@
         for d, other in enumerate(group_peers, 1)
     ]
     stage_c = [exchange(plane, plane, {"wide": sibling}, all_nodes.at[group, other_half])]
-    lax.fori_loop(1, 3, two_leaves, 0)
+    lax.fori_loop(2, 4, two_leaves, 0)
     finish(stage_c)
     local[4].wait()
 
@@ -292,15 +299,21 @@
     stage_r = [
         exchange(tree.at[0], roots.at[d], {"narrow": other}) for d, other in enumerate(group_peers)
     ]
-    lax.fori_loop(3, 6, two_leaves, 0)
-    finish(stage_d)
-    stage_e = []
-    for d in range(1, groups):
-        other = in_groups(d)
+
+    def pass_on(d):
+        other = in_groups(groups - d)
         block = all_nodes.at[other, pl.ds(half, chips)]
-        stage_e.append(
-            exchange(block, block, {"wide": sibling}, all_nodes.at[other, other_half])
-        )
+        mirrored = all_nodes.at[other, other_half]
+        return exchange(block, block, {"wide": sibling}, mirrored)
+
+    close = [d for d in range(1, groups) if d in (1, groups - 1)]
+    distant = [d for d in range(1, groups) if d not in close]
+    lax.fori_loop(4, 5, two_leaves, 0)
+    finish([stage_d[d - 1] for d in close])
+    stage_e = [pass_on(d) for d in close]
+    lax.fori_loop(5, 7, two_leaves, 0)
+    finish([stage_d[d - 1] for d in distant])
+    stage_e += [pass_on(d) for d in distant]
     finish(stage_r)
     target = tree[0][rhs:]
     field = None
@@ -312,44 +325,25 @@
         start = lax.rem(lax.div(me, 1 << section), 2) * skel_count
         matrix = top_here[place, pl.ds(pl.multiple_of(start, skel_count), skel_count), :]
         field = times_transposed(field, matrix)
-    field_out[...] = field
-    lax.fori_loop(6, leaves // 2, two_leaves, 0)
+    top_field[...] = field
+    lax.fori_loop(7, leaves // 2, two_leaves, 0)
     finish(stage_e)
     target = all_nodes[group, slot][rhs:]
-    field = field_out[...]
+    field = top_field[...]
     for i in range(far_list.shape[1]):
         e = far_list[0, i]
         place = lax.rem(e, wide)
         source = all_nodes[lax.div(e, wide), lax.rem(place, 2) * chips + lax.div(place, 2)]
         field = field + node_field(source, target, rhs)
-    field_out[...] = field
-
-
-def down_kernel(
-    field, transfer, basis, near_out, out, transfer_here, basis_here, near_here, sem
-):
-    leaves, rhs, box = near_out.shape
-    skel_count = basis.shape[2]
-    copies = [
-        pltpu.make_async_copy(src, dst, sem.at[i])
-        for i, (src, dst) in enumerate(
-            ((transfer, transfer_here), (basis, basis_here), (near_out, near_here))
-        )
-    ]
-    for copy in copies:
-        copy.start()
-    copies[0].wait()
-    fields = [field[...]]
+    fields = [field]
     while len(fields) < leaves:
         parents = len(fields)
         both = [times_transposed(fields[p], transfer_here[parents - 1 + p]) for p in range(parents)]
         fields = [half for pair in both for half in (pair[:, :skel_count], pair[:, skel_count:])]
-    copies[1].wait()
-    copies[2].wait()
     scale = 1.0 / math.sqrt(box)
     for leaf in range(leaves):
         far_part = times_transposed(fields[leaf], basis_here[leaf])
-        out[leaf] = ((near_here[leaf] + far_part) * scale).astype(BF16)
+        out[leaf] = ((near_out[leaf] + far_part) * scale).astype(BF16)
 
 
 def shards(
@@ -370,12 +364,13 @@
     size = (rhs + dims, skel)
     side = math.isqrt(wide // 2)
     copies = 4 + 2 * (side - 1) + 1 + 3 * (groups - 1)
-    field, near_out = pl.pallas_call(
+    out = pl.pallas_call(
         main_kernel,
-        out_shape=(shape(F32, rhs, skel), shape(F32, leaves, rhs, box)),
+        out_shape=shape(BF16, leaves, rhs, box),
         in_specs=[smem] * 2 + [anywhere] * 5 + [vmem] * 3,
-        out_specs=(vmem, vmem),
+        out_specs=vmem,
         scratch_shapes=[
+            pltpu.VMEM((leaves, rhs, box), F32),
             pltpu.VMEM((3, *points.shape), BF16),
             pltpu.VMEM((3 * leaves, rhs, box), BF16),
             pltpu.VMEM(basis.shape, BF16),
@@ -385,6 +380,7 @@
             pltpu.VMEM((groups, wide, *size), F32),
             pltpu.VMEM((wide - 1, *size), F32),
             pltpu.VMEM((groups - 1, *size), F32),
+            pltpu.VMEM((rhs, skel), F32),
             pltpu.VMEM((3 * leaves, box, 32), BF16),
             pltpu.VMEM((leaves, 32, box), BF16),
             pltpu.VMEM((box, box), BF16),
@@ -401,20 +397,6 @@
         near_list[0].T, far_list[0], points, charges, basis, local_transfer[0], top_transfer[0],
         leaf_skeleton[0], jnp.swapaxes(local_skeleton, 0, 1), jnp.swapaxes(top_skeleton, 0, 1),
     )
-    out = pl.pallas_call(
-        down_kernel,
-        out_shape=shape(BF16, leaves, rhs, box),
-        in_specs=[vmem] + [anywhere] * 3,
-        out_specs=vmem,
-        scratch_shapes=[
-            pltpu.VMEM(local_transfer.shape[1:], BF16),
-            pltpu.VMEM(basis.shape, BF16),
-            pltpu.VMEM((leaves, rhs, box), F32),
-            pltpu.SemaphoreType.DMA((3,)),
-        ],
-        compiler_params=pltpu.CompilerParams(vmem_limit_bytes=VMEM_BYTES),
-        name="down",
-    )(field, local_transfer[0], basis, near_out)
     return out[None]
 
 

time: 56.3 us -> 57.9 us (1.028)
  local copies, waits for them, and re-layouts: 0 us -> 1.88 us
    unnamed x0 -> x1, local copies, waits for them, and re-layouts: none -> 1.88 us
    pallas_call x2 -> x1, Pallas kernels: 55.7 us -> 55.8 us  [shards(): pl.pallas_call(main_kernel, out_shape=shape(BF16, leaves, rhs, box), in_s...]
where the time goes in v4:
time: 57.9 us; the launch traced here: 57.7 us
  Pallas kernels  55.8 us (96%)
  local copies, waits for them, and re-layouts  1.88 us (3%)
    pallas_call x1, Pallas kernels, shards(): pl.pallas_call(main_kernel, out_shape=shape(BF16, leaves, rhs, box), in_s...  55.8 us
    unnamed x1, local copies, waits for them, and re-layouts  1.88 us

profile of v4, /device:TPU:0, one launch (start us, length us, event | category | flops | bytes accessed | tf_op | source)
XLA Modules:
  0.0 57.7 jit_solution(13020087835537281473)
XLA Ops:
  0.0 55.8 %main.1 = bf16[16,32,512]{2,1,0:T(8,128)(2,1)} custom-call(s32[8,16]{1,0:T(8,128)} %bitcast.22, s32[1,4]{1,0:T(1,128)} %bitcast.23, bf16[16,8,512]{2,1,0:T(8,128)(2,1)} %bitcast.18, bf16[16,32,512]{2,1,0:T(8,128)(2,1)} %bitcast.17, bf16[16,512,128]{2,1,0:T(8,128)(2,1)} %bitcast.14, bf16[15,256,128]{2,1,0:T(8,128)(2,1)} %bitcast.16, ...), custom_call_target="tpu_custom_call" | custom-call | tf_op jit(solution)/shard_map/main/pallas_call | solution.py:367
  55.8 1.9 %copy.12 = bf16[1,16,32,512]{3,2,1,0:T(8,128)(2,1)} copy(bf16[1,16,32,512]{3,2,1,0:T(8,128)(2,1)} %bitcast.13) | data formatting | bytes 1048576

commit v5 on v4

--- a/solution.py
+++ b/solution.py
@@ -306,14 +306,9 @@
         mirrored = all_nodes.at[other, other_half]
         return exchange(block, block, {"wide": sibling}, mirrored)
 
-    close = [d for d in range(1, groups) if d in (1, groups - 1)]
-    distant = [d for d in range(1, groups) if d not in close]
-    lax.fori_loop(4, 5, two_leaves, 0)
-    finish([stage_d[d - 1] for d in close])
-    stage_e = [pass_on(d) for d in close]
-    lax.fori_loop(5, 7, two_leaves, 0)
-    finish([stage_d[d - 1] for d in distant])
-    stage_e += [pass_on(d) for d in distant]
+    lax.fori_loop(4, 7, two_leaves, 0)
+    finish(stage_d)
+    stage_e = [pass_on(d) for d in range(1, groups)]
     finish(stage_r)
     target = tree[0][rhs:]
     field = None

time: 57.9 us -> 53.6 us (0.926)
  Pallas kernels: 55.8 us -> 51.5 us
    pallas_call x1, Pallas kernels: 55.8 us -> 51.5 us  [shards(): pl.pallas_call(main_kernel, out_shape=shape(BF16, leaves, rhs, box), in_s...]
where the time goes in v5:
time: 53.6 us; the launch traced here: 53.3 us
  Pallas kernels  51.5 us (96%)
  local copies, waits for them, and re-layouts  1.88 us (4%)
    pallas_call x1, Pallas kernels, shards(): pl.pallas_call(main_kernel, out_shape=shape(BF16, leaves, rhs, box), in_s...  51.5 us
    unnamed x1, local copies, waits for them, and re-layouts  1.88 us

profile of v5, /device:TPU:0, one launch (start us, length us, event | category | flops | bytes accessed | tf_op | source)
XLA Modules:
  0.0 53.3 jit_solution(15464458506377213271)
XLA Ops:
  0.0 51.5 %main.1 = bf16[16,32,512]{2,1,0:T(8,128)(2,1)} custom-call(s32[8,16]{1,0:T(8,128)} %bitcast.22, s32[1,4]{1,0:T(1,128)} %bitcast.23, bf16[16,8,512]{2,1,0:T(8,128)(2,1)} %bitcast.18, bf16[16,32,512]{2,1,0:T(8,128)(2,1)} %bitcast.17, bf16[16,512,128]{2,1,0:T(8,128)(2,1)} %bitcast.14, bf16[15,256,128]{2,1,0:T(8,128)(2,1)} %bitcast.16, ...), custom_call_target="tpu_custom_call" | custom-call | tf_op jit(solution)/shard_map/main/pallas_call | solution.py:362
  51.5 1.9 %copy.12 = bf16[1,16,32,512]{3,2,1,0:T(8,128)(2,1)} copy(bf16[1,16,32,512]{3,2,1,0:T(8,128)(2,1)} %bitcast.13) | data formatting | bytes 1048576

commit v6 on v5

--- a/solution.py
+++ b/solution.py
@@ -15,6 +15,7 @@
 LAST_DIMS = (((1,), (1,)), ((), ()))
 FIRST_DIMS = (((0,), (0,)), ((), ()))
 VMEM_BYTES = 56 * 2**20
+EARLY = 2
 
 
 def dot(a, b, dims=(((1,), (0,)), ((), ()))):
@@ -84,7 +85,7 @@
     near_list, far_list, points, charges, basis, transfer, top_transfer, leaf_skel, skel, top_skel,
     out,
     near_out, near_points, near_charges, basis_here, transfer_here, top_here, nodes, all_nodes, tree, roots, top_field,
-    sources, targets, kernel_a, kernel_b, local_sem, send_sem, recv_sem,
+    sources, targets, kernel_a, kernel_b, early, local_sem, send_sem, recv_sem,
 ):
     leaves, rhs, box = charges.shape
     skel_count = basis.shape[2]
@@ -226,18 +227,7 @@
     fill_own(0, kernel_a)
     lax.fori_loop(0, leaves // 4, own_pair, 0)
     finish(halo_points)
-    lax.fori_loop(leaves // 4, 3 * leaves // 8, own_pair_and_halo, 0)
-    finish(stage_a)
-    line = all_nodes.at[group, pl.ds(half + row * side, side)]
-    stage_b = [
-        exchange(
-            line, line, {"wide": other},
-            all_nodes.at[group, pl.ds(half + in_column(side - d) * side, side)],
-        )
-        for d, other in enumerate(column_peers, 1)
-    ]
-    lax.fori_loop(3 * leaves // 8, leaves // 2, own_pair_and_halo, 0)
-    finish(halo_charges)
+    lax.fori_loop(leaves // 4, leaves // 2, own_pair_and_halo, 0)
     first_leaf = (me - 1) * leaves
 
     def place_of(leaf, k):
@@ -260,8 +250,33 @@
                 near_out[leaf] = total
         return carry
 
-    fill(0, 1, kernel_a)
-    lax.fori_loop(0, 2, two_leaves, 0)
+    def fill_leaf(leaf, carry):
+        for k in range(1, near):
+            fill(leaf, k, early.at[leaf * (near - 1) + k - 1])
+        return carry
+
+    def use_leaf(leaf, carry):
+        total = near_out[leaf]
+        for k in range(1, near):
+            block = early[leaf * (near - 1) + k - 1]
+            total = total + dot(near_charges[place_of(leaf, k)], block)
+        near_out[leaf] = total
+        return carry
+
+    lax.fori_loop(0, EARLY, fill_leaf, 0)
+    finish(stage_a)
+    line = all_nodes.at[group, pl.ds(half + row * side, side)]
+    stage_b = [
+        exchange(
+            line, line, {"wide": other},
+            all_nodes.at[group, pl.ds(half + in_column(side - d) * side, side)],
+        )
+        for d, other in enumerate(column_peers, 1)
+    ]
+    finish(halo_charges)
+    lax.fori_loop(0, EARLY, use_leaf, 0)
+    fill(EARLY, 1, kernel_a)
+    lax.fori_loop(EARLY // 2, 2, two_leaves, 0)
     finish(stage_b)
     plane = all_nodes.at[group, pl.ds(half, chips)]
     other_half = pl.ds((1 - core) * chips, chips)
@@ -380,6 +395,7 @@
             pltpu.VMEM((leaves, 32, box), BF16),
             pltpu.VMEM((box, box), BF16),
             pltpu.VMEM((box, box), BF16),
+            pltpu.VMEM((EARLY * (near_list.shape[2] - 1), box, box), BF16),
             pltpu.SemaphoreType.DMA((5,)),
             pltpu.SemaphoreType.DMA((copies,)),
             pltpu.SemaphoreType.DMA((copies,)),

time: 53.6 us -> 51.4 us (0.959)
  Pallas kernels: 51.5 us -> 49 us
    pallas_call x1, Pallas kernels: 51.5 us -> 49 us  [shards(): pl.pallas_call(main_kernel, out_shape=shape(BF16, leaves, rhs, box), in_s...]
where the time goes in v6:
time: 51.4 us; the launch traced here: 50.9 us
  Pallas kernels  49 us (95%)
  local copies, waits for them, and re-layouts  1.88 us (4%)
    pallas_call x1, Pallas kernels, shards(): pl.pallas_call(main_kernel, out_shape=shape(BF16, leaves, rhs, box), in_s...  49 us
    unnamed x1, local copies, waits for them, and re-layouts  1.88 us

profile of v6, /device:TPU:0, one launch (start us, length us, event | category | flops | bytes accessed | tf_op | source)
XLA Modules:
  0.0 50.9 jit_solution(8564256171444152067)
XLA Ops:
  0.0 49.0 %main.1 = bf16[16,32,512]{2,1,0:T(8,128)(2,1)} custom-call(s32[8,16]{1,0:T(8,128)} %bitcast.22, s32[1,4]{1,0:T(1,128)} %bitcast.23, bf16[16,8,512]{2,1,0:T(8,128)(2,1)} %bitcast.18, bf16[16,32,512]{2,1,0:T(8,128)(2,1)} %bitcast.17, bf16[16,512,128]{2,1,0:T(8,128)(2,1)} %bitcast.14, bf16[15,256,128]{2,1,0:T(8,128)(2,1)} %bitcast.16, ...), custom_call_target="tpu_custom_call" | custom-call | tf_op jit(solution)/shard_map/main/pallas_call | solution.py:377
  49.0 1.9 %copy.12 = bf16[1,16,32,512]{3,2,1,0:T(8,128)(2,1)} copy(bf16[1,16,32,512]{3,2,1,0:T(8,128)(2,1)} %bitcast.13) | data formatting | bytes 1048576
